TPU v7x, 32 devices: a whole 2x2x4 slice. The times are simulated.
32 devices in a mesh: dp: 16 (over z, y, x), tensor: 2 (over core).
Axes of the slice: x: 2, y: 2, z: 4, core: 2. Of those that a mesh axis runs over, the one named last changes fastest.
Arguments:
- tokens: bfloat16 [16384, 768], P('dp'), may hold values from -6 to 6
- upper_delta: bfloat16 [16384, 768], P(('dp', 'tensor')), may hold values from -0.119628906 to 0.119628906
- segments: int32 [32, 512], P('dp'), may hold values from 0 to 3, as said below
- summary_index: int32 [32, 4], P('dp'), may hold values from 0 to 419, as said below
- validity: int32 [32, 512], P('dp'), may hold values from 0 to 1, as said below
- queries: bfloat16 [128, 768], P('dp'), may hold values from -15 to 15
- positives: int32 [128], P('dp'), may hold values from 0 to 127
- query_weight: bfloat16 [768, 768], P(None, 'tensor'), may hold values from -0.21875 to 0.21875
- key_weight: bfloat16 [768, 768], P(None, 'tensor'), may hold values from -0.21875 to 0.21875
- value_weight: bfloat16 [768, 768], P(None, 'tensor'), may hold values from -0.21875 to 0.21875
- query_bias: bfloat16 [768], P('tensor'), may hold values from -3 to 3
- value_bias: bfloat16 [768], P('tensor'), may hold values from -3 to 3
- output_weight: bfloat16 [768, 768], P('tensor'), may hold values from -1.25 to 1.25
- output_bias: bfloat16 [768], replicated, may hold values from -3 to 3
- first_gain: bfloat16 [768], replicated, may hold values from 0.25 to 1.75
- first_shift: bfloat16 [768], replicated, may hold values from -3 to 3
- up_weight: bfloat16 [768, 3072], P(None, 'tensor'), may hold values from -0.21875 to 0.21875
- up_bias: bfloat16 [3072], P('tensor'), may hold values from -3 to 3
- down_weight: bfloat16 [3072, 768], P('tensor'), may hold values from -0.109375 to 0.109375
- down_bias: bfloat16 [768], replicated, may hold values from -3 to 3
- second_gain: bfloat16 [768], replicated, may hold values from 0.25 to 1.75
Outputs:
- loss_terms: float32 [128], P('dp')
- query_gradient: float32 [128, 768], P('dp')
- token_gradient: bfloat16 [16384, 768], P(('dp', 'tensor'))
- query_weight_gradient: float32 [768, 768], P(None, 'tensor')
- key_weight_gradient: float32 [768, 768], P(None, 'tensor')
- value_weight_gradient: float32 [768, 768], P(None, 'tensor')
- query_bias_gradient: float32 [768], P('tensor')
- value_bias_gradient: float32 [768], P('tensor')
- output_weight_gradient: float32 [768, 768], P('tensor')
- output_bias_gradient: float32 [768], replicated
- first_gain_gradient: float32 [768], replicated
- first_shift_gradient: float32 [768], replicated
- up_weight_gradient: float32 [768, 3072], P(None, 'tensor')
- up_bias_gradient: float32 [3072], P('tensor')
- down_weight_gradient: float32 [3072, 768], P('tensor')
- down_bias_gradient: float32 [768], replicated
- second_gain_gradient: float32 [768], replicated
Inputs may be any that keep to these rules, and one draw needn't show every extreme that they name: `segments`: along each row the numbers never fall; every one of the 4 passages of a row holds at least an eighth of 512 consecutive tokens, and padding tokens carry the last passage's number. `summary_index`: each entry is a valid token of passage k of its row, among that passage's first four tokens. `validity`: each row ends in a run of 1 to 64 padding tokens that lies inside its last passage; all other tokens are 1.
All inputs are finite; a program needn't handle non-finite values.
Results may differ from a plain program's by a relative error of at most 0.04.
Values may be sent and summed in bfloat16 or wider, within the bound.
No kernel may reach another device: no remote copies, remote signals or barrier semaphores. Data moves between devices by JAX's collectives and lax.ppermute only.
A program may use at most 192 MiB of HBM per device.

v0:
```python
import functools
import math

import jax
import jax.numpy as jnp
from jax import lax
from jax.experimental import pallas as pl
from jax.experimental.pallas import tpu as pltpu
from jax.sharding import PartitionSpec as P

D = 768
HD = 64
LANES = 128

norm_eps = 1e-05
neg_large = -1e30
root_half = 0.7071067811865476
inv_root_tau = 0.3989422804014327
log2_e = 1.4426950408889634

f32, bf16 = jnp.float32, jnp.bfloat16
COSTS = dict(
    attend_far=8, attend_near=7, forward=15, loss_back=4,
    unit_back_far=4, unit_back_near=0.4, down_gradient=3, up_gradient=0.16,
    first_back=1.8, attend_back_near=3.5, attend_back_far=3.5, head_gradients=5,
    down_add_halves=2, down_add_quarters=2, down_add_eighths=2, down_add_last=2,
    down_join_pieces=2, down_join_eighths=2, down_join_quarters=2, down_finish_down=6,
    up_add_halves=2, up_add_quarters=2, up_add_eighths=2, up_add_last=2,
    up_join_pieces=2, up_join_eighths=2, up_join_quarters=2, up_finish_up=6,
    heads_add_halves=2, heads_add_quarters=2, heads_add_eighths=2, heads_add_last=2,
    heads_join_pieces=2, heads_join_eighths=6, heads_join_quarters=2, heads_finish_heads=8,
)
FLOPS = int(1.15e+09)
SMALL = 16


def bits_of(axis):
    return lax.axis_size(axis).bit_length() - 1


def flip_by(value, axis, mask):
    size = lax.axis_size(axis)
    return lax.ppermute(value, axis, [(i, i ^ mask) for i in range(size)])


def swap(value):
    return flip_by(value, "tensor", 1)


def dot(left, right):
    return jnp.dot(left, right, preferred_element_type=f32)


def dot_t(left, right):
    return lax.dot_general(left, right, (((1,), (1,)), ((), ())), preferred_element_type=f32)


def t_dot(left, right):
    return lax.dot_general(left, right, (((0,), (0,)), ((), ())), preferred_element_type=f32)


class Late:
    def __init__(self, source, held, semaphore):
        self.held, self.waited = held, False
        self.shape, self.dtype = held.shape, held.dtype
        self.copy = pltpu.make_async_copy(source, held, semaphore)
        self.copy.start()

    def wait(self):
        if not self.waited:
            self.copy.wait()
        self.waited = True
        return self.held


class Early:
    def __init__(self, held, target, semaphore):
        self.held, self.target, self.semaphore, self.sent = held, target, semaphore, False
        self.shape, self.dtype = held.shape, held.dtype

    def __getitem__(self, at):
        return self.held[at]

    def __setitem__(self, at, value):
        self.held[at] = value

    def send(self, *at):
        source, target = (self.held.at[at], self.target.at[at]) if at else (self.held, self.target)
        pltpu.make_async_copy(source, target, self.semaphore).start()
        self.sent = True

    def finish(self):
        if not self.sent:
            self.send()
        pltpu.make_async_copy(self.held, self.target, self.semaphore).wait()


def ready(*values):
    return [value.wait() if isinstance(value, Late) else value for value in values]


def call(kernel, name, outs, *args, scratch=(), late=(), early=(), order=None, grant=20, final=()):
    after = order or []
    count, waits, made = len(args), len(after), len(outs)
    held = [pltpu.VMEM(args[i].shape, args[i].dtype) for i in late] + [pltpu.VMEM(*outs[i]) for i in early]
    args = [pltpu.with_memory_space_constraint(a, pltpu.HBM) if i in late else a for i, a in enumerate(args)]

    def body(*refs):
        inputs = list(refs[:count])
        results = list(refs[count + waits : count + waits + made])
        rest = refs[count + waits + made :]
        scratches, rest = rest[: len(scratch)], rest[len(scratch) :]
        for k, i in enumerate(late):
            inputs[i] = Late(inputs[i], rest[k], rest[-1].at[k])
        for k, i in enumerate(early, len(late)):
            results[i] = Early(rest[k], results[i], rest[-1].at[k])
        kernel(*inputs, *results, *scratches)
        for i in early:
            results[i].finish()

    specs = [pl.BlockSpec(memory_space=pltpu.SMEM)]
    specs += [pl.BlockSpec(memory_space=pltpu.HBM if i in late else pltpu.VMEM) for i in range(1, count)]
    specs += [pl.BlockSpec(memory_space=pl.ANY)] * waits
    own = [pltpu.SemaphoreType.DMA((len(held),))] if held else []
    made_by = pl.pallas_call(
        body,
        name=name,
        out_shape=[
            jax.ShapeDtypeStruct(*out) if i in final else (pltpu.HBM if i in early else pltpu.VMEM)(*out)
            for i, out in enumerate(outs)
        ],
        in_specs=specs,
        out_specs=[pl.BlockSpec(memory_space=pltpu.HBM if i in early else pltpu.VMEM) for i in range(made)],
        scratch_shapes=[*scratch, *held, *own],
        compiler_params=pltpu.CompilerParams(vmem_limit_bytes=grant << 20),
        cost_estimate=pl.CostEstimate(
            flops=int(COSTS[name] * FLOPS), bytes_accessed=1, transcendentals=0
        ),
    )(*args, *after)
    if order is not None:
        order[:] = [made_by[-1]]
    return made_by


def rows_at(index, size):
    return pl.ds(pl.multiple_of(index * size, size), size)


def add_low(left, right):
    return (left.astype(f32) + right.astype(f32)).astype(bf16)


BX, BY, BZ, BT, BD, PLACES = range(6)


def add_halves(info, keep_a, came_a, keep_b, came_b, send_a, kept_a, send_b, kept_b):
    quarter = keep_b.shape[0] // 2
    for bit, keep, came, send, kept in (
        (info[BY], keep_a, came_a, send_a, kept_a),
        (info[BX], keep_b, came_b, send_b, kept_b),
    ):
        mine, other = rows_at(bit, quarter), rows_at(1 - bit, quarter)
        send[:quarter] = add_low(keep[other], came[other])
        kept[:quarter] = add_low(keep[mine], came[mine])
        if keep.shape[0] > 2 * quarter:
            extra = add_low(keep[2 * quarter :], came[2 * quarter :])
            send[quarter:] = extra
            kept[quarter:] = extra


def add_quarters(info, keep_a, came_a, keep_b, came_b, send, kept):
    quarter, width = keep_b.shape[0], keep_a.shape[1]
    half = quarter // 2
    bit = info[BZ] & 1
    for out, side in ((send, 1 - bit), (kept, bit)):
        at = rows_at(side, half)
        out[:half, :width] = add_low(keep_a[at], came_a[at])
        out[:half, width:] = add_low(keep_b[at], came_b[at])
        if keep_a.shape[0] > quarter:
            out[half:, :width] = add_low(keep_a[quarter:], came_a[quarter:])
            out[half:, width:] = jnp.zeros((out.shape[0] - half, out.shape[1] - width), bf16)


def add_eighths(info, keep, came, send, kept, *, half):
    bit = info[BZ] >> 1
    for out, side in ((send, 1 - bit), (kept, bit)):
        at = rows_at(side, half)
        out[:half] = add_low(keep[at], came[at])
        if kept.shape[0] > half:
            out[half:] = add_low(keep[2 * half :], came[2 * half :])


def add_last(info, keep, came, total, *small):
    size = total.shape[0]
    total[...] = add_low(keep[:size], came[:size])
    if small:
        small[0][...] = add_low(keep[size:], came[size:])


def join_pieces(info, own, came, eighth):
    size = own.shape[0]
    bit = info[BZ] >> 1
    eighth[rows_at(bit, size)] = own[...]
    eighth[rows_at(1 - bit, size)] = came[...]


def join_eighths(info, own, came, quarter_a, quarter_b):
    size, width = own.shape[0], quarter_a.shape[1]
    bit = info[BZ] & 1
    for source, side in ((own, bit), (came, 1 - bit)):
        quarter_a[rows_at(side, size)] = source[:, :width]
        quarter_b[rows_at(side, size)] = source[:, width:]


def join_quarters(info, own_a, came_a, own_b, came_b, half_a, half_b):
    size = own_a.shape[0]
    for bit, own, came, half in (
        (info[BY], own_a, came_a, half_a),
        (info[BX], own_b, came_b, half_b),
    ):
        half[rows_at(bit, size)] = own[...]
        half[rows_at(1 - bit, size)] = came[...]


def finish_down(info, own_a, came_a, own_b, came_b, out, mark):
    mark[...] = jnp.zeros_like(mark)
    size = own_a.shape[0]
    for part, bit, own, came in ((0, info[BX], own_a, came_a), (1, info[BY], own_b, came_b)):
        for side, source in ((bit, own), (1 - bit, came)):
            at = rows_at(2 * part + side, size)
            out[at] = source[...].astype(f32)
            out.send(at)


def put(out, rows, columns, value):
    at = rows, pl.ds(columns, value.shape[1])
    out[at] = value.astype(f32)
    out.send(*at)


def finish_up(info, own_a, came_a, own_b, came_b, up, output, mark):
    mark[...] = jnp.zeros_like(mark)
    size, width = own_a.shape
    rest = up.shape[1] - width
    for side, source in ((info[BX], own_a), (1 - info[BX], came_a)):
        put(up, rows_at(side, size), 0, source[...])
    for side, source in ((info[BY], own_b), (1 - info[BY], came_b)):
        put(up, rows_at(side, size), width, source[:, :rest])
        at = slice(None), rows_at(side, size)
        output[at] = source[:, rest:].astype(f32)
        output.send(*at)


def finish_heads(info, own_a, came_a, own_b, came_b, query, key, value):
    size, width = own_a.shape
    own = query.shape[1]
    rest = width - own
    for side, source in ((info[BX], own_a), (1 - info[BX], came_a)):
        put(query, rows_at(side, size), 0, source[:, :own])
        put(key, rows_at(side, size), 0, source[:, own:])
    for side, source in ((info[BY], own_b), (1 - info[BY], came_b)):
        put(key, rows_at(side, size), rest, source[:, : own - rest])
        put(value, rows_at(side, size), 0, source[:, own - rest :])


class Reduction:
    def __init__(self, name, info, order):
        self.name, self.info, self.order = name, info, order

    def begin(self, halves):
        self.made = halves
        send_a, send_b, self.keep_a, self.keep_b = halves
        self.came = [flip_by(send_a, "dp", 1), flip_by(send_b, "dp", 2)]

    def staged(self, kernel, outs, *args, early=(), **fixed):
        bound = functools.partial(kernel, **fixed) if fixed else kernel
        self.made = call(bound, self.name + kernel.__name__, outs, self.info, *args, order=self.order, early=early)
        return self.made

    def quarters(self):
        (first, self.wide), (half, self.narrow) = self.keep_a.shape, self.keep_b.shape
        self.extra, self.quarter = first - half, half // 2
        a, b = ((self.quarter + self.extra, self.wide), bf16), ((self.quarter, self.narrow), bf16)
        send_a, self.keep_a, send_b, self.keep_b = self.staged(
            add_halves, [a, a, b, b], self.keep_a, self.came[0], self.keep_b, self.came[1]
        )
        self.came = [flip_by(send_a, "dp", 2), flip_by(send_b, "dp", 1)]

    def eighths(self):
        self.both = self.wide + self.narrow
        piece = ((self.quarter // 2 + self.extra, self.both), bf16)
        send, self.own = self.staged(
            add_quarters, [piece] * 2, self.keep_a, self.came[0], self.keep_b, self.came[1]
        )
        self.came = flip_by(send, "dp", 4)

    def pieces(self):
        size = self.quarter // 4
        piece = ((size + self.extra, self.both), bf16)
        send, self.own = self.staged(add_eighths, [piece] * 2, self.own, self.came, half=size)
        self.came = flip_by(send, "dp", 8)

    def total(self):
        outs = [((self.quarter // 4, self.both), bf16)]
        outs += [((self.extra, self.both), bf16)] if self.extra else []
        self.own, *small = [
            functools.reduce(
                lambda value, bit: add_low(value, flip_by(value, "dp", 1 << bit)),
                range(4, bits_of("dp")),
                made,
            )
            for made in self.staged(add_last, outs, self.own, self.came)
        ]
        self.small = small[0] if small else None
        self.came = flip_by(self.own, "dp", 8)

    def join_two_z(self):
        piece = ((self.quarter // 2, self.both), bf16)
        (self.own,) = self.staged(join_pieces, [piece], self.own, self.came)
        self.came = flip_by(self.own, "dp", 4)

    def join_z(self):
        outs = [((self.quarter, self.wide), bf16), ((self.quarter, self.narrow), bf16)]
        self.keep_a, self.keep_b = self.staged(join_eighths, outs, self.own, self.came)
        self.came = [flip_by(self.keep_a, "dp", 2), flip_by(self.keep_b, "dp", 1)]

    def join_two(self):
        outs = [((2 * self.quarter, self.wide), bf16), ((2 * self.quarter, self.narrow), bf16)]
        self.keep_a, self.keep_b = self.staged(
            join_quarters, outs, self.keep_a, self.came[0], self.keep_b, self.came[1]
        )
        self.came = [flip_by(self.keep_a, "dp", 1), flip_by(self.keep_b, "dp", 2)]

    def finish(self, kernel, outs):
        return self.staged(
            kernel, outs, self.keep_a, self.came[0], self.keep_b, self.came[1],
            early=[i for i, out in enumerate(outs) if out[0][0] > 8],
        )


def down_gradient(info, unit, active, unit_in, active_in, send_a, send_b, keep_a, keep_b):
    size = send_a.shape[0]
    unit, active, unit_in, active_in = ready(unit, active, unit_in, active_in)
    for side in range(2):
        for part, bit, outs in ((0, info[BX], (send_a, keep_a)), (1, info[BY], (send_b, keep_b))):
            at = rows_at(2 * part + (bit if side else 1 - bit), size)
            outs[side][...] = (
                t_dot(active[:, at], unit[...]) + t_dot(active_in[:, at], unit_in[...])
            ).astype(bf16)


def up_gradient(
    info, delta, first, delta_in, first_in, branch, branch_far, context, context_far, send_a, send_b, keep_a, keep_b,
    bias,
):
    size, width = send_a.shape
    rest = delta.shape[1] - width
    for side in range(2):
        for bit, outs, columns in (
            (info[BX], (send_a, keep_a), pl.ds(0, width)),
            (info[BY], (send_b, keep_b), pl.ds(width, rest)),
        ):
            at = rows_at(bit if side else 1 - bit, size)
            out = outs[side]
            out[:, : columns.size] = (
                t_dot(first[:, at], delta[:, columns]) + t_dot(first_in[:, at], delta_in[:, columns])
            ).astype(bf16)
            if columns.size == rest:
                out[:, rest:] = (dot(context[...], branch[:, at]) + dot(context_far[...], branch_far[:, at])).astype(
                    bf16
                )
    ones = jnp.ones((8, delta.shape[0]), bf16)
    bias[...] = dot(ones, delta[...]) + dot(ones, delta_in[...])


def head_gradients(
    info, tokens, query, query_far, key, key_far, value, value_far, shared, shared_in, bias, send_a, send_b, keep_a,
    keep_b,
):
    half, width = send_b.shape[0], send_a.shape[1]
    length, narrow = query.shape
    rest = width - narrow
    near, far = rows_at(info[BT], length), rows_at(1 - info[BT], length)
    for side in range(2):
        for bit, outs, sources in (
            (info[BX], (send_a, keep_a), ((query, query_far, 0, narrow), (key, key_far, 0, rest))),
            (info[BY], (send_b, keep_b), ((key, key_far, rest, narrow - rest), (value, value_far, 0, narrow))),
        ):
            at = rows_at(bit if side else 1 - bit, half)
            tokens_near, tokens_far = tokens[near, at], tokens[far, at]
            put_at = 0
            for left, right, first, count in sources:
                columns = pl.ds(first, count)
                outs[side][:half, pl.ds(put_at, count)] = (
                    t_dot(tokens_near, left[:, columns]) + t_dot(tokens_far, right[:, columns])
                ).astype(bf16)
                put_at += count
    ones = jnp.ones((8, length), bf16)
    query_sum = dot(ones, query[...]) + dot(ones, query_far[...])
    value_sum = dot(ones, value[...]) + dot(ones, value_far[...])
    sums = shared[...] + shared_in[...]
    pairs = [(sums[k : k + 1, :narrow], sums[k : k + 1, narrow:]) for k in range(5)]
    pairs += [(bias[:1, k * narrow : (k + 1) * narrow], bias[:1, (k + 1) * narrow : (k + 2) * narrow]) for k in (0, 2)]
    pairs += [(query_sum[:1], value_sum[:1])]
    block = jnp.concatenate([piece for pair in pairs for piece in pair], 0)
    block = jnp.concatenate([block, jnp.zeros((SMALL, rest), f32)], 1).astype(bf16)
    send_a[half:] = block
    keep_a[half:] = block


def attend(
    info, tokens, query_weight, key_weight, value_weight, query_bias, value_bias, segments, validity,
    context, query, key, value, raised, shares, shade, *, far,
):
    length = context.shape[1]
    row = 1 - info[BT] if far else info[BT]
    segments, validity = ready(segments, validity)
    mark = segments[pl.ds(row, 1)]
    seen = jnp.where(validity[pl.ds(row, 1)] > 0, mark, -1)
    column = jnp.broadcast_to(seen.astype(f32), (8, length)).T[:, :1]
    shade[...] = jnp.where(column == mark.astype(f32), 0.0, neg_large)
    tokens, query_weight, query_bias, value_bias = ready(tokens, query_weight, query_bias, value_bias)
    x = tokens[rows_at(row, length)]
    scale = 1.0 / math.sqrt(HD)
    query[...] = (
        (dot(x, query_weight[...]) + query_bias[...].astype(f32)[None]).astype(bf16) * bf16(scale)
    )
    query.send()
    (key_weight,) = ready(key_weight)
    key[...] = dot(x, key_weight[...]).astype(bf16)
    key.send()
    (value_weight,) = ready(value_weight)
    value[...] = (dot(x, value_weight[...]) + value_bias[...].astype(f32)[None]).astype(bf16)
    value.send()
    low = lax.broadcasted_iota(jnp.int32, (length, LANES), 1) < HD

    def body(pair, _):
        at = pl.ds(pl.multiple_of(pair * LANES, LANES), LANES)
        q, k, v = query[:, at], key[:, at], value[:, at]

        def logits_of(member):
            return dot_t(k, jnp.where(low if member == 0 else ~low, q, jnp.zeros_like(q))) + shade[...]

        coming = logits_of(0)
        for member in range(2):
            logits, coming = coming, logits_of(1) if member == 0 else None
            number = 2 * pair + member
            peak = jnp.max(logits, 0, keepdims=True)
            lifted = jnp.exp(logits - peak).astype(bf16)
            raised[number] = lifted
            raised.send(number)
            sums = t_dot(jnp.where(low if member == 0 else ~low, v, jnp.ones_like(v)), lifted)
            other = (1 - member) * HD
            share = 1.0 / sums[other : other + 1]
            shares[pl.ds(number, 1)] = share
            rows = pl.ds(pl.multiple_of(number * HD, HD), HD)
            context[rows] = (sums[member * HD : member * HD + HD] * share).astype(bf16)
            context.send(rows)
        return 0

    lax.fori_loop(0, context.shape[0] // LANES, body, 0)


def attend_back(
    info, branch, output_weight, shares, value, context, raised, key, query, query_weight, key_weight, value_weight,
    query_delta, key_delta, value_delta, part, context_delta,
):
    length = part.shape[0]
    branch, output_weight = ready(branch, output_weight)
    context_delta[...] = dot_t(output_weight[...], branch[...]).astype(bf16)
    value, context, raised, key, query = ready(value, context, raised, key, query)
    low = lax.broadcasted_iota(jnp.int32, (length, LANES), 1) < HD
    scale = 1.0 / math.sqrt(HD)

    def body(pair, _):
        at = pl.ds(pl.multiple_of(pair * LANES, LANES), LANES)
        queries, keys, values = [], [], []
        for member in range(2):
            rows = pl.ds(pl.multiple_of(pair * LANES + member * HD, HD), HD)
            delta = context_delta[rows].astype(f32) * shares[pl.ds(2 * pair + member, 1)]
            inner = jnp.sum(delta * context[rows].astype(f32), 0, keepdims=True)
            delta = delta.astype(bf16)
            none = jnp.zeros_like(delta)
            delta = jnp.concatenate([none, delta] if member else [delta, none], 0)
            lifted = raised[2 * pair + member]
            logit_delta = (lifted.astype(f32) * (dot(value[:, at], delta) - inner)).astype(bf16)
            values.append(dot_t(lifted, delta))
            keys.append(dot(logit_delta, query[:, at]))
            queries.append(t_dot(key[:, at], logit_delta)[member * HD : member * HD + HD])
        query_delta[:, at] = (jnp.concatenate(queries, 0) * scale).T.astype(bf16)
        key_delta[:, at] = jnp.where(low, keys[0], keys[1]).astype(bf16)
        value_delta[:, at] = (values[0] + values[1]).astype(bf16)
        return 0

    lax.fori_loop(0, query.shape[1] // LANES, body, 0)
    query_weight, key_weight, value_weight = ready(query_weight, key_weight, value_weight)
    part[...] = (
        dot_t(query_delta[...], query_weight[...])
        + dot_t(key_delta[...], key_weight[...])
        + dot_t(value_delta[...], value_weight[...])
    ).astype(part.dtype)


OB, FG, FS, DB, SG = range(5)


def center(inputs):
    shifted = inputs - jnp.mean(inputs, -1, keepdims=True)
    spread = jnp.mean(shifted * shifted, -1, keepdims=True)
    row_scale = lax.rsqrt(spread + norm_eps)
    return shifted * row_scale, row_scale


def norm_back(out_delta, normed, row_scale, norm_gain):
    scaled = out_delta * norm_gain
    first_mean = jnp.mean(scaled, -1, keepdims=True)
    second_mean = jnp.mean(scaled * normed, -1, keepdims=True)
    return row_scale * (scaled - first_mean - normed * second_mean)


def forward(
    info, context, output_near, tokens, context_in, output_far, up_far, down_far, up_near, down_near, vectors,
    bias_near, bias_far, first_low, first_normed, first_scale, active_near, active_far, slope_near, slope_far,
    second_normed, second_scale, summary, total,
):
    length = total.shape[0]
    step = length // 2
    halves = (pl.ds(0, step), pl.ds(step, step))
    base = info[BT] * length
    context, output_near, tokens = ready(context, output_near, tokens)
    for at in halves:
        heads = t_dot(context[:, at], output_near[...]) + t_dot(context_in[:, at], output_far[...])
        x = tokens[pl.ds(pl.multiple_of(base + at.start, step), step)].astype(f32)
        normed, scale = center(x + (heads + vectors[OB : OB + 1]))
        out = normed * vectors[FG : FG + 1] + vectors[FS : FS + 1]
        first_normed[at] = normed.astype(bf16)
        first_scale[at] = scale
        first_low[at] = out.astype(bf16)
        total[at] = out + vectors[DB : DB + 1]
    first_low.send()
    first_normed.send()
    first_scale.send()

    width = 6 * LANES
    groups = (
        (up_far, down_far, bias_far, active_far, slope_far),
        (up_near, down_near, bias_near, active_near, slope_near),
    )
    for up, down, bias, active, slope in groups:
        up, down = ready(up, down)

        def body(index, _, up=up, down=down, bias=bias, active=active, slope=slope):
            units = rows_at(index, width)

            def hidden_of(at):
                return dot(first_low[at], up[:, units]) + bias[:, units]

            coming = hidden_of(halves[0])
            for at in halves:
                hidden, coming = coming, hidden_of(halves[1]) if at is halves[0] else None
                share = 0.5 * (1.0 + lax.erf(hidden * root_half))
                low = (hidden * share).astype(bf16)
                active[at, units] = low
                slope[at, units] = (share + hidden * jnp.exp(-0.5 * hidden * hidden) * inv_root_tau).astype(bf16)
                total[at] += dot(low, down[units])
            active.send(slice(None), units)
            slope.send(slice(None), units)
            return 0

        lax.fori_loop(0, bias.shape[1] // width, body, 0)

    for at in halves:
        normed, scale = center(total[at])
        second_normed[at] = normed.astype(bf16)
        second_scale[at] = scale
        total[at] = normed * vectors[SG : SG + 1]
    rows = [total[pl.ds(info[PLACES + k], 1)] for k in range(summary.shape[0])]
    summary[...] = jnp.concatenate(rows, 0).astype(bf16)


def loss_back(
    info, near, far, upper, normed, scale, vectors, losses, query_gradient, second_delta, unit_delta, sums, all_rows,
    out_delta,
):
    width = upper.shape[1]
    all_rows[: near.shape[0]] = near[...]
    all_rows[near.shape[0] :] = far[...]
    here = info[BT] * near.shape[0] + info[BD] * 8
    places = near.shape[0] // 8
    count = all_rows.shape[0]
    block = min(256, count)
    score_scale = 1.0 / math.sqrt(width)
    own_passages = 4

    def body(index, sums_in):
        at = rows_at(index, block)
        rows = all_rows[at, :width]
        digits = all_rows[at, width:].astype(f32)
        scores = dot_t(rows, all_rows[:, :width]) * score_scale
        columns = lax.broadcasted_iota(jnp.int32, (block, count), 1) ^ here
        numbers = (lax.broadcasted_iota(jnp.int32, (block, 1), 0) + index * block) ^ here
        scores = jnp.where((columns & 7) < own_passages, scores, neg_large)
        peak = jnp.max(scores, -1, keepdims=True)
        raised = jnp.exp(scores - peak)
        total = jnp.sum(raised, -1, keepdims=True)
        target = (digits[:, 0:1] * 16.0 + digits[:, 1:2]).astype(jnp.int32)
        chosen = columns == target
        lost = peak + jnp.log(total) - jnp.sum(jnp.where(chosen, scores, 0.0), -1, keepdims=True)
        delta = raised / total - chosen.astype(f32)
        delta = jnp.where((numbers & 7) >= own_passages, delta, 0.0).astype(bf16)
        wide = delta.astype(f32)
        places_here = lax.broadcasted_iota(jnp.int32, (block, 8), 1)
        wanted = ((places_here >> 2) * places + info[BD]) * 8 + own_passages + (places_here & 3)
        mine = (numbers == wanted).astype(f32)
        own_losses = sums_in[0] + jnp.sum(mine * lost, 0, keepdims=True)
        own_delta = sums_in[1] + t_dot(mine.astype(bf16), delta)
        results = []
        for k in range(own_passages):
            column = (info[BT] * places + info[BD]) * 8 + k
            share = jnp.sum(jnp.where(columns == column, wide, 0.0), -1, keepdims=True)
            results.append(sums_in[2 + k] + jnp.sum(share * rows.astype(f32), 0, keepdims=True))
        return own_losses, own_delta, *results

    zero = jnp.zeros((1, width), f32)
    first = (jnp.zeros((1, 8), f32), jnp.zeros((8, count), f32), *[zero] * own_passages)
    if count == block:
        own_losses, own_delta, *passage_delta = body(0, first)
    else:
        own_losses, own_delta, *passage_delta = lax.fori_loop(0, count // block, body, first)
    upper, normed, scale = ready(upper, normed, scale)
    out_delta[...] = upper[...].astype(f32)
    for k in range(own_passages):
        out_delta[pl.ds(info[PLACES + k], 1)] += passage_delta[k] * score_scale
    query_gradient[...] = dot(own_delta.astype(bf16), all_rows[:, :width]) * score_scale
    losses[...] = own_losses

    length = upper.shape[0]
    step = length // 4
    bias_sum = gain_sum = zero
    for start in range(0, length, step):
        at = pl.ds(start, step)
        n = normed[at].astype(f32)
        delta = norm_back(out_delta[at], n, scale[at], vectors[SG : SG + 1])
        unit_delta[at] = delta.astype(bf16)
        second_delta[at] = delta
        bias_sum += jnp.sum(delta, 0, keepdims=True)
        gain_sum += jnp.sum(out_delta[at] * n, 0, keepdims=True)
    sums[...] = jnp.concatenate(
        [jnp.zeros((DB, width), f32), bias_sum, gain_sum, jnp.zeros((7 - SG, width), f32)], 0
    )


def unit_back(info, unit_delta, down_weight, slope, hidden_delta):
    width = 6 * LANES

    def body(index, _):
        units = rows_at(index, width)
        delta = dot_t(unit_delta[...], down_weight[units])
        hidden_delta[:, units] = (delta * slope[:, units].astype(f32)).astype(bf16)
        return 0

    lax.fori_loop(0, down_weight.shape[0] // width, body, 0)


def first_back(
    info, delta_far, up_far, delta_near, up_near, second_delta, normed, scale, vectors, sums_in, first_delta,
    branch, sums, total,
):
    length, width = total.shape
    delta_far, up_far = ready(delta_far, up_far)
    total[...] = dot_t(delta_far[...], up_far[...])
    delta_near, up_near = ready(delta_near, up_near)
    total[...] += dot_t(delta_near[...], up_near[...])
    second_delta, normed = ready(second_delta, normed)
    step = length // 4
    zero = jnp.zeros((1, width), f32)
    bias_sum = gain_sum = shift_sum = zero
    for start in range(0, length, step):
        at = pl.ds(start, step)
        out_delta = second_delta[at] + total[at]
        n = normed[at].astype(f32)
        delta = norm_back(out_delta, n, scale[at], vectors[FG : FG + 1])
        branch[at] = delta.astype(bf16)
        first_delta[at] = delta
        bias_sum += jnp.sum(delta, 0, keepdims=True)
        gain_sum += jnp.sum(out_delta * n, 0, keepdims=True)
        shift_sum += jnp.sum(out_delta, 0, keepdims=True)
    sums[...] = sums_in[...] + jnp.concatenate(
        [bias_sum, gain_sum, shift_sum, jnp.zeros((7 - FS, width), f32)], 0
    )


def shards(
    tokens,
    upper_delta,
    segments,
    summary_index,
    validity,
    queries,
    positives,
    query_weight,
    key_weight,
    value_weight,
    query_bias,
    value_bias,
    output_weight,
    output_bias,
    first_gain,
    first_shift,
    up_weight,
    up_bias,
    down_weight,
    down_bias,
    second_gain,
):
    row_count, length = segments.shape
    token_count = row_count * length
    members = lax.axis_size("tensor")
    place = lax.axis_index("tensor")
    own_count = token_count // members
    width_local = query_weight.shape[1]
    heads_local = width_local // HD
    at_dp = lax.axis_index("dp")
    half_rows = D // 2

    def own(value):
        part = value.shape[0] // members
        return lax.dynamic_slice_in_dim(value, place * part, part, 0)

    info = jnp.concatenate(
        [
            jnp.stack([at_dp & 1, (at_dp >> 1) & 1, (at_dp >> 2) & 3, place, at_dp]).astype(jnp.int32),
            own(summary_index).reshape(-1),
        ]
    )
    vectors = jnp.stack([output_bias, first_gain, first_shift, down_bias, second_gain]).astype(f32)
    vectors = jnp.concatenate([vectors, jnp.zeros((3, D), f32)], 0)
    output_far = swap(output_weight)
    up_far = swap(up_weight)
    bias_far = swap(up_bias.reshape(1, -1))
    down_far = swap(down_weight)

    context_shape = ((length, width_local), bf16)

    def attention(far):
        return call(
            functools.partial(attend, far=far),
            "attend_far" if far else "attend_near",
            [((width_local, length), bf16)] + [context_shape] * 3
            + [((heads_local, length, length), bf16), ((heads_local + -heads_local % 8, length), f32)],
            info, tokens, query_weight, key_weight, value_weight, query_bias, value_bias, segments, validity,
            scratch=[pltpu.VMEM((length, length), f32)],
            late=(1, 2, 3, 4, 5, 6, 7, 8) if far else (),
            early=(0, 1, 2, 3, 4, 5),
        )

    context_far, query_far, key_far, value_far, raised_far, shares_far = attention(True)
    context_in = swap(context_far)
    context, query, key, value, raised, shares = attention(False)

    row, units = ((length, D), bf16), ((length, up_weight.shape[1]), bf16)
    scale_shape = ((length, 1), f32)
    own_passages = summary_index.shape[1]
    (
        first_low, first_normed, first_scale, active, active_far, slope, slope_far, second_normed, second_scale,
        summary,
    ) = call(
        forward, "forward",
        [row, row, scale_shape, units, units, units, units, row, scale_shape, ((own_passages, D), bf16)],
        info, context, output_weight, tokens, context_in, output_far, up_far, down_far, up_weight, down_weight,
        vectors, up_bias.reshape(1, -1).astype(f32), bias_far.astype(f32),
        late=(1, 2, 3, 7, 8, 9), early=(0, 1, 2, 3, 4, 5, 6, 7, 8), grant=40,
        scratch=[pltpu.VMEM((length, D), f32)],
    )
    first_in = swap(first_low)
    active_in = swap(active_far)

    places = lax.axis_size("dp")
    row_of = ((positives % 8) // 4 * places + positives // 8) * 8 + positives % 4
    digits = jnp.stack([row_of // 16, row_of % 16], 1).astype(bf16)
    digits = jnp.pad(digits, ((0, 0), (0, LANES - 2)))
    bundle = jnp.concatenate(
        [jnp.pad(summary, ((0, 0), (0, LANES))), own(jnp.concatenate([queries, digits], 1))], 0
    )
    for low in (1, 4):
        bundle = jnp.concatenate([bundle, *[flip_by(bundle, "dp", low * k) for k in (1, 2, 3)]], 0)
    for bit in range(4, bits_of("dp")):
        bundle = jnp.concatenate([bundle, flip_by(bundle, "dp", 1 << bit)], 0)
    bundle_far = swap(bundle)
    gathered = 2 * bundle.shape[0]
    query_count = queries.shape[0]
    losses, query_gradient, second_delta, unit_delta, sums = call(
        loss_back, "loss_back",
        [((1, query_count), f32), ((query_count, D), f32), ((length, D), f32), row, ((8, D), f32)],
        info, bundle, bundle_far, upper_delta, second_normed, second_scale, vectors,
        late=(3, 4, 5), final=(0, 1), grant=20 if gathered <= 256 else 50,
        scratch=[pltpu.VMEM((gathered, D + LANES), bf16), pltpu.VMEM((length, D), f32)],
    )
    unit_in = swap(unit_delta)
    order = []

    def through_units(name, weight, slope):
        return call(
            unit_back, name, [units], info, unit_delta, weight, slope, order=order
        )[0]

    delta_far = through_units("unit_back_far", down_far, slope_far)
    delta_in = swap(delta_far)
    down, up, heads = [Reduction(name, info, order) for name in ("down_", "up_", "heads_")]
    held = {}
    wide_shape, mark = (query_weight.shape, f32), ((8, LANES), f32)
    down.begin(
        call(
            down_gradient, "down_gradient", [((half_rows, D), bf16)] * 4, info, unit_delta, active, unit_in, active_in,
            order=order,
        )
    )

    def two_parts(columns, extra=0):
        wide = (columns // 2 + LANES - 1) // LANES * LANES
        first, second = ((half_rows + extra, wide), bf16), ((half_rows, columns - wide), bf16)
        return [first, second, first, second]

    def near_units():
        held["delta"] = through_units("unit_back_near", down_weight, slope)

    def first_norm():
        held["first_delta"], held["branch"], held["shared"] = call(
            first_back, "first_back", [((length, D), f32), row, ((8, D), f32)], info, delta_far, up_far,
            held["delta"], up_weight, second_delta, first_normed, first_scale, vectors, sums,
            scratch=[pltpu.VMEM((length, D), f32)], order=order,
        )
        held["branch_far"], held["shared_in"] = swap(held["branch"]), swap(held["shared"])

    def up_begin():
        *halves, held["bias"] = call(
            up_gradient, "up_gradient",
            two_parts(up_weight.shape[1] + width_local) + [((8, up_weight.shape[1]), f32)],
            info, held["delta"], first_low, delta_in, first_in, held["branch"], held["branch_far"], context,
            context_far, order=order,
        )
        up.begin(halves)

    def attention_back(name, branch, shares, raised, query, key, value, context, kind):
        return call(
            attend_back,
            name,
            [context_shape] * 3 + [((length, D), kind)],
            info, branch, output_weight, shares, value, context, raised, key, query, query_weight, key_weight,
            value_weight,
            scratch=[pltpu.VMEM((width_local, length), bf16)],
            order=order,
        )

    def near_row():
        held["near"] = attention_back(
            "attend_back_near", held["branch"], shares, raised, query, key, value, context, f32
        )

    def far_row():
        held["far"] = attention_back(
            "attend_back_far", held["branch_far"], shares_far, raised_far, query_far, key_far, value_far, context_far,
            bf16,
        )
        held["part_in"] = swap(held["far"][3])

    def heads_begin():
        near, far = held["near"], held["far"]
        heads.begin(
            call(
                head_gradients, "head_gradients", two_parts(3 * width_local, SMALL), info, tokens, near[0], far[0],
                near[1], far[1], near[2], far[2], held["shared"], held["shared_in"], held["bias"], order=order,
            )
        )

    up_outs = [(up_weight.shape, f32), (output_weight.shape, f32), mark]
    stages = [
        near_units, first_norm, up_begin, down.quarters, near_row, down.eighths,
        far_row, up.quarters, down.pieces, heads_begin, down.total, up.eighths,
        heads.quarters, down.join_two_z, up.pieces, heads.eighths, down.join_z, up.total,
        heads.pieces, up.join_two_z, down.join_two, heads.total, up.join_z, heads.join_two_z,
        up.join_two, heads.join_z, down.finish, heads.join_two, up.finish,
    ]
    for stage in stages:
        if stage == down.finish:
            down_total = stage(finish_down, [(down_weight.shape, f32), mark])[0]
        elif stage == up.finish:
            up_total, output_total, _ = stage(finish_up, up_outs)
        else:
            stage()
    heads_total = heads.finish(finish_heads, [wide_shape] * 3)
    small_total = heads.small[:, :width_local].astype(f32).reshape(8, -1)
    token_gradient = (held["first_delta"] + held["near"][3] + held["part_in"].astype(f32)).astype(bf16)

    return (
        losses.reshape(-1),
        query_gradient,
        token_gradient,
        heads_total[0],
        heads_total[1],
        heads_total[2],
        small_total[7, :width_local],
        small_total[7, width_local:],
        output_total,
        small_total[OB],
        small_total[FG],
        small_total[FS],
        up_total,
        small_total[5:7].reshape(-1),
        down_total,
        small_total[DB],
        small_total[SG],
    )


def solution(mesh):
    in_specs = (
        P("dp", None),
        P(("dp", "tensor"), None),
        P("dp", None),
        P("dp", None),
        P("dp", None),
        P("dp", None),
        P("dp"),
        P(None, "tensor"),
        P(None, "tensor"),
        P(None, "tensor"),
        P("tensor"),
        P("tensor"),
        P("tensor", None),
        P(),
        P(),
        P(),
        P(None, "tensor"),
        P("tensor"),
        P("tensor", None),
        P(),
        P(),
    )
    out_specs = (
        P("dp"),
        P("dp", None),
        P(("dp", "tensor"), None),
        P(None, "tensor"),
        P(None, "tensor"),
        P(None, "tensor"),
        P("tensor"),
        P("tensor"),
        P("tensor", None),
        P(),
        P(),
        P(),
        P(None, "tensor"),
        P("tensor"),
        P("tensor", None),
        P(),
        P(),
    )
    return jax.shard_map(shards, mesh=mesh, in_specs=in_specs, out_specs=out_specs, check_vma=False)
```

profile of v0, /device:TPU:0, one launch (start us, length us, event | category | flops | bytes accessed | tf_op | source)
XLA Modules:
  0.0 221.2 jit_solution(14859342055644065630)
XLA Ops:
  1.5 9.3 %attend_far.1 = (bf16[384,512]{1,0:T(8,128)(2,1)}, bf16[512,384]{1,0:T(8,128)(2,1)}, bf16[512,384]{1,0:T(8,128)(2,1)}, bf16[512,384]{1,0:T(8,128)(2,1)}, bf16[6,512,512]{2,1,0:T(8,128)(2,1)}, /*index=5*/f32[8,512]{1,0:T(8,128)}) custom-call(s32[9]{0:T(128)S(1)} %concatenate.22.refs_0_, bf16[1024,768]{1,0:T(8,128)(2,1)} %refs_1_.5, bf16[768,384]{1,0:T(8,128)(2,1)} %refs_9_.5, ...), custom_call_target="tpu_custom_call" | custom-call | flops 9200000000 | bytes 1 | tf_op jit(solution)/shard_map/attend_far/pallas_call | solution.py:125
  12.1 6.6 %attend_near.1 = (bf16[384,512]{1,0:T(8,128)(2,1)}, bf16[512,384]{1,0:T(8,128)(2,1)}, bf16[512,384]{1,0:T(8,128)(2,1)}, bf16[512,384]{1,0:T(8,128)(2,1)}, bf16[6...) custom-call(s32[9]{0:T(128)S(1)} %concatenate.22.refs_0_, bf16[1024,768]{1,0:T(8,128)(2,1)S(1)} %copy-done.10, ...), custom_call_target="tpu_custom_call" | custom-call | flops 8049999872 | bytes 1 | tf_op jit(solution)/shard_map/attend_near/pallas_call | solution.py:125
  19.2 13.3 %forward.1 = (bf16[512,768]{1,0:T(8,128)(2,1)}, bf16[512,768]{1,0:T(8,128)(2,1)}, f32[512,1]{1,0:T(8,128)}, bf16[512,1536]{1,0:T(8,128)(2,1)}, bf16[512,1536]{1,...) custom-call(s32[9]{0:T(128)S(1)} %concatenate.22.refs_0_, ...), custom_call_target="tpu_custom_call" | custom-call | flops 17250000896 | bytes 1 | tf_op jit(solution)/shard_map/forward/pallas_call | solution.py:125
  32.6 3.0 %collective-permute-start.5 = (bf16[8,896]{1,0:T(8,128)(2,1)S(1)}, bf16[8,896]{1,0:T(8,128)(2,1)S(1)}, u32[]{:S(2)}, u32[]{:S(2)}) collective-permute-start(bf16[8,896]{1,0:T(8,128)(2,1)S(1)} %pad_maximum_fusion), channel_id=1, source_target_pairs={{0,2},{2,0},{4,6},{6,4},{8,10},{10,8},{12,14},{14,12},{16,18},{18,... | collective-permute-start | bytes 43016 | tf_op jit(solution)/shard_map/ppermute | solution.py:43
  35.6 1.5 collective-permute-start.6
  37.3 2.0 collective-permute-done.6
  39.3 2.4 %collective-permute-done.7 = bf16[8,896]{1,0:T(8,128)(2,1)S(1)} collective-permute-done((bf16[8,896]{1,0:T(8,128)(2,1)S(1)}, bf16[8,896]{1,0:T(8,128)(2,1)S(1)}, u32[]{:S(2)}, u32[]{:S(2)}) %collective-permute-start.7) | collective-permute-done | bytes 14368 | tf_op jit(solution)/shard_map/ppermute | solution.py:43
  41.8 3.7 %collective-permute-start.10 = (bf16[32,896]{1,0:T(8,128)(2,1)S(1)}, bf16[32,896]{1,0:T(8,128)(2,1)S(1)}, u32[]{:S(2)}, u32[]{:S(2)}) collective-permute-start(bf16[32,896]{1,0:T(8,128)(2,1)S(1)} %concatenate.27), channel_id=1, source_target_pairs={{0,24},{2,26},{4,28},{6,30},{8,16},{10,18},{12,20},{14,22},{16,8},... | collective-permute-start | bytes 172040 | tf_op jit(solution)/shard_map/ppermute | solution.py:43
  46.3 1.7 collective-permute-done.10
  48.0 1.7 collective-permute-done.8
  49.7 0.9 collective-permute-done.9
  50.8 1.5 collective-permute-done.11.refs_2_
  52.2 3.6 %loss_back.1 = (f32[1,8]{1,0:T(1,128)}, f32[8,768]{1,0:T(8,128)}, f32[512,768]{1,0:T(8,128)S(1)}, bf16[512,768]{1,0:T(8,128)(2,1)S(1)}, f32[8,768]{1,0:T(8,128)S(1)}) custom-call(s32[9]{0:T(128)S(1)} %concatenate.22.refs_0_, bf16[128,896]{1,0:T(8,128)(2,1)S(1)} %concatenate.28.refs_1_, bf16[128,896]{1,0:T(8,128)(2,1)S(1)} %collective-permute-done.11.refs_2_, ...), custom_call_target="tpu_custom_call" | custom-call | flops 4600000000 | bytes 1 | tf_op jit(solution)/shard_map/loss_back/pallas_call | solution.py:125
  56.0 3.6 %unit_back_far.1.refs_5_.refs_1_ = bf16[512,1536]{1,0:T(8,128)(2,1)S(1)} custom-call(s32[9]{0:T(128)S(1)} %concatenate.22.refs_0_, bf16[512,768]{1,0:T(8,128)(2,1)S(1)} %get-tuple-element.121.refs_1_, bf16[1536,768]{1,0:T(8,128)(2,1)} %collective-permute-done.3.refs_7_.refs_2_, bf16[512,1536]{1,0:T(8,128)(2,1)S(1)} %copy-done.28), custom_call_target="tpu_custom_call" | custom-call | flops 4600000000 | bytes 1 | tf_op jit(solution)/shard_map/unit_back_far/pallas_call | solution.py:125
  60.3 4.3 %down_gradient.1 = (bf16[384,768]{1,0:T(8,128)(2,1)S(1)}, bf16[384,768]{1,0:T(8,128)(2,1)S(1)}, bf16[384,768]{1,0:T(8,128)(2,1)S(1)}, bf16[384,768]{1,0:T(8,128)(2,1)S(1)}) custom-call(s32[9]{0:T(128)S(1)} %concatenate.22.refs_0_, bf16[512,768]{1,0:T(8,128)(2,1)S(1)} %get-tuple-element.121.refs_1_, bf16[512,1536]{1,0:T(8,128)(2,1)S(1)} %copy-done.27, ...), custom_call_target="tpu_custom_call" | custom-call | flops 3449999872 | bytes 1 | tf_op jit(solution)/shard_map/down_gradient/pallas_call | solution.py:125
  64.6 2.2 unit_back_near.1.refs_3_.refs_10_.refs_1_
  66.9 3.8 %first_back.1 = (f32[512,768]{1,0:T(8,128)S(1)}, bf16[512,768]{1,0:T(8,128)(2,1)S(1)}, f32[8,768]{1,0:T(8,128)S(1)}) custom-call(s32[9]{0:T(128)S(1)} %concatenate.22.refs_0_, bf16[512,1536]{1,0:T(8,128)(2,1)S(1)} %unit_back_far.1.refs_5_.refs_1_, bf16[768,1536]{1,0:T(8,128)(2,1)S(1)} %collective-permute-done.2.refs_6_.refs_2_, ...), custom_call_target="tpu_custom_call" | custom-call | flops 2070000000 | bytes 1 | tf_op jit(solution)/shard_map/first_back/pallas_call | solution.py:125
  73.1 4.4 %up_gradient.1 = (bf16[384,1024]{1,0:T(8,128)(2,1)S(1)}, bf16[384,896]{1,0:T(8,128)(2,1)S(1)}, bf16[384,1024]{1,0:T(8,128)(2,1)S(1)}, bf16[384,896]{1,0:T(8,128)(2,1)S(1)}, f32[8,1536]{1,0:T(8,128)S(1)}) custom-call(s32[9]{0:T(128)S(1)} %concatenate.22.refs_0_, bf16[512,1536]{1,0:T(8,128)(2,1)S(1)} %unit_back_near.1.refs_3_.refs_10_.refs_1_, ...), custom_call_target="tpu_custom_call" | custom-call | flops 184000000 | bytes 1 | tf_op jit(solution)/shard_map/up_gradient/pallas_call | solution.py:125
  77.5 9.1 %collective-permute-done.14.refs_2_ = bf16[384,768]{1,0:T(8,128)(2,1)S(1)} collective-permute-done((bf16[384,768]{1,0:T(8,128)(2,1)S(1)}, bf16[384,768]{1,0:T(8,128)(2,1)S(1)}, u32[]{:S(2)}, u32[]{:S(2)}) %collective-permute-start.14) | collective-permute-done | bytes 589856 | tf_op jit(solution)/shard_map/ppermute | solution.py:43
  88.3 1.5 collective-permute-start.20
  90.3 1.5 collective-permute-start.25
  91.9 6.7 %attend_back_near.1 = (bf16[512,384]{1,0:T(8,128)(2,1)S(1)}, bf16[512,384]{1,0:T(8,128)(2,1)S(1)}, bf16[512,384]{1,0:T(8,128)(2,1)S(1)}, f32[512,768]{1,0:T(8,128)S(1)}) custom-call(s32[9]{0:T(128)S(1)} %concatenate.22.refs_0_, bf16[512,768]{1,0:T(8,128)(2,1)S(1)} %get-tuple-element.132.refs_5_.refs_1_, bf16[384,768]{1,0:T(8,128)(2,1)} %refs_2_.11, ...), custom_call_target="tpu_custom_call" | custom-call | flops 4024999936 | bytes 1 | tf_op jit(solution)/shard_map/attend_back_near/pallas_call | solution.py:125
  99.4 2.1 collective-permute-start.23
  101.5 7.0 %attend_back_far.1 = (bf16[512,384]{1,0:T(8,128)(2,1)S(1)}, bf16[512,384]{1,0:T(8,128)(2,1)S(1)}, bf16[512,384]{1,0:T(8,128)(2,1)S(1)}, bf16[512,768]{1,0:T(8,128)(2,1)S(1)}) custom-call(s32[9]{0:T(128)S(1)} %concatenate.22.refs_0_, bf16[512,768]{1,0:T(8,128)(2,1)S(1)} %collective-permute-done.18.refs_6_.refs_1_, bf16[384,768]{1,0:T(8,128)(2,1)} %refs_2_.11, ...), custom_call_target="tpu_custom_call" | custom-call | flops 4024999936 | bytes 1 | tf_op jit(solution)/shard_map/attend_back_far/pallas_call | solution.py:125
  108.6 1.9 collective-permute-done.25.refs_4_
  110.5 2.3 %collective-permute-done.24.refs_2_ = bf16[384,1024]{1,0:T(8,128)(2,1)S(1)} collective-permute-done((bf16[384,1024]{1,0:T(8,128)(2,1)S(1)}, bf16[384,1024]{1,0:T(8,128)(2,1)S(1)}, u32[]{:S(2)}, u32[]{:S(2)}) %collective-permute-start.24) | collective-permute-done | bytes 786464 | tf_op jit(solution)/shard_map/ppermute | solution.py:43
  114.3 1.3 collective-permute-start.30
  115.6 1.5 collective-permute-start.28
  117.2 1.4 collective-permute-start.29
  118.6 3.4 %head_gradients.1 = (bf16[400,640]{1,0:T(8,128)(2,1)S(1)}, bf16[384,512]{1,0:T(8,128)(2,1)S(1)}, bf16[400,640]{1,0:T(8,128)(2,1)S(1)}, bf16[384,512]{1,0:T(8,128)(2,1)S(1)}) custom-call(s32[9]{0:T(128)S(1)} %concatenate.22.refs_0_, bf16[1024,768]{1,0:T(8,128)(2,1)S(1)} %copy-done.11, bf16[512,384]{1,0:T(8,128)(2,1)S(1)} %get-tuple-element.156.refs_2_, ...), custom_call_target="tpu_custom_call" | custom-call | flops 5750000128 | bytes 1 | tf_op jit(solution)/shard_map/head_gradients/pallas_call | solution.py:125
  122.7 0.9 collective-permute-start.27
  124.2 1.3 collective-permute-start.34
  125.5 1.2 add_convert_fusion
  128.0 1.5 collective-permute-start.33
  129.6 3.1 %collective-permute-done.27.refs_4_ = bf16[384,512]{1,0:T(8,128)(2,1)S(1)} collective-permute-done((bf16[384,512]{1,0:T(8,128)(2,1)S(1)}, bf16[384,512]{1,0:T(8,128)(2,1)S(1)}, u32[]{:S(2)}, u32[]{:S(2)}) %collective-permute-start.27) | collective-permute-done | bytes 393248 | tf_op jit(solution)/shard_map/ppermute | solution.py:43
  132.6 2.8 %collective-permute-done.26.refs_2_ = bf16[400,640]{1,0:T(8,128)(2,1)S(1)} collective-permute-done((bf16[400,640]{1,0:T(8,128)(2,1)S(1)}, bf16[400,640]{1,0:T(8,128)(2,1)S(1)}, u32[]{:S(2)}, u32[]{:S(2)}) %collective-permute-start.26) | collective-permute-done | bytes 512032 | tf_op jit(solution)/shard_map/ppermute | solution.py:43
  136.7 1.4 collective-permute-start.32
  138.7 1.1 collective-permute-start.37
  140.5 2.7 %collective-permute-start.36 = (bf16[48,1920]{1,0:T(8,128)(2,1)S(1)}, bf16[48,1920]{1,0:T(8,128)(2,1)S(1)}, u32[]{:S(2)}, u32[]{:S(2)}) collective-permute-start(bf16[48,1920]{1,0:T(8,128)(2,1)S(1)} %get-tuple-element.186), channel_id=1, source_target_pairs={{0,16},{2,18},{4,20},{6,22},{8,24},{10,26},{12,28},{14,30},{16,0},... | collective-permute-start | bytes 552968 | tf_op jit(solution)/shard_map/ppermute | solution.py:43
  144.5 5.9 %collective-permute-done.37.refs_2_ = bf16[96,1536]{1,0:T(8,128)(2,1)S(1)} collective-permute-done((bf16[96,1536]{1,0:T(8,128)(2,1)S(1)}, bf16[96,1536]{1,0:T(8,128)(2,1)S(1)}, u32[]{:S(2)}, u32[]{:S(2)}) %collective-permute-start.37) | collective-permute-done | bytes 294944 | tf_op jit(solution)/shard_map/ppermute | solution.py:43
  151.0 2.4 %collective-permute-start.39 = (bf16[192,768]{1,0:T(8,128)(2,1)S(1)}, bf16[192,768]{1,0:T(8,128)(2,1)S(1)}, u32[]{:S(2)}, u32[]{:S(2)}) collective-permute-start(bf16[192,768]{1,0:T(8,128)(2,1)S(1)} %get-tuple-element.190.refs_1_), channel_id=1, source_target_pairs={{0,4},{2,6},{4,0},{6,2},{8,12},{10,14},{12,8},{14,10},{16,20},{18,... | collective-permute-start | bytes 884744 | tf_op jit(solution)/shard_map/ppermute | solution.py:43
  153.4 2.2 collective-permute-start.40
  157.0 2.9 %collective-permute-start.38 = (bf16[64,1152]{1,0:T(8,128)(2,1)S(1)}, bf16[64,1152]{1,0:T(8,128)(2,1)S(1)}, u32[]{:S(2)}, u32[]{:S(2)}) collective-permute-start(bf16[64,1152]{1,0:T(8,128)(2,1)S(1)} %get-tuple-element.189), channel_id=1, source_target_pairs={{0,16},{2,18},{4,20},{6,22},{8,24},{10,26},{12,28},{14,30},{16,0},... | collective-permute-start | bytes 442376 | tf_op jit(solution)/shard_map/ppermute | solution.py:43
  159.9 6.5 %collective-permute-done.41.refs_2_ = bf16[48,1920]{1,0:T(8,128)(2,1)S(1)} collective-permute-done((bf16[48,1920]{1,0:T(8,128)(2,1)S(1)}, bf16[48,1920]{1,0:T(8,128)(2,1)S(1)}, u32[]{:S(2)}, u32[]{:S(2)}) %collective-permute-start.41) | collective-permute-done | bytes 184352 | tf_op jit(solution)/shard_map/ppermute | solution.py:43
  168.4 1.4 collective-permute-done.38.refs_2_
  170.3 1.1 collective-permute-start.42
  171.4 3.0 %collective-permute-done.43.refs_2_ = bf16[96,1920]{1,0:T(8,128)(2,1)S(1)} collective-permute-done((bf16[96,1920]{1,0:T(8,128)(2,1)S(1)}, bf16[96,1920]{1,0:T(8,128)(2,1)S(1)}, u32[]{:S(2)}, u32[]{:S(2)}) %collective-permute-start.43) | collective-permute-done | bytes 368672 | tf_op jit(solution)/shard_map/ppermute | solution.py:43
  174.5 1.3 up_join_eighths.1
  175.8 1.0 collective-permute-start.46
  180.3 1.3 squeeze.23
  185.1 2.1 collective-permute-done.45.refs_2_
  187.1 1.2 up_join_quarters.1
  188.3 1.6 collective-permute-start.54
  190.0 0.9 copy-done.18
  190.9 1.0 heads_join_eighths.1
  192.9 1.6 collective-permute-start.53
  194.5 2.8 %down_finish_down.1 = (f32[1536,768]{1,0:T(8,128)}, f32[8,128]{1,0:T(8,128)S(1)}) custom-call(s32[9]{0:T(128)S(1)} %concatenate.22.refs_0_, bf16[384,768]{1,0:T(8,128)(2,1)S(1)} %get-tuple-element.199.refs_1_, bf16[384,768]{1,0:T(8,128)(2,1)S(1)} %collective-permute-done.49.refs_2_, bf16[384,768]{1,0:T(8,128)(2,1)S(1)} %get-tuple-element.191.refs_3_, ...), custom_call_target="tpu_custom_call" | custom-call | flops 6899999744 | bytes 1 | tf_op jit(solution)/shard_map/down_finish_down/pallas_call | solution.py:125
  197.3 2.4 %collective-permute-done.48.refs_4_ = bf16[192,512]{1,0:T(8,128)(2,1)S(1)} collective-permute-done((bf16[192,512]{1,0:T(8,128)(2,1)S(1)}, bf16[192,512]{1,0:T(8,128)(2,1)S(1)}, u32[]{:S(2)}, u32[]{:S(2)}) %collective-permute-start.48) | collective-permute-done | bytes 196640 | tf_op jit(solution)/shard_map/ppermute | solution.py:43
  199.7 8.9 %collective-permute-done.47.refs_2_ = bf16[192,640]{1,0:T(8,128)(2,1)S(1)} collective-permute-done((bf16[192,640]{1,0:T(8,128)(2,1)S(1)}, bf16[192,640]{1,0:T(8,128)(2,1)S(1)}, u32[]{:S(2)}, u32[]{:S(2)}) %collective-permute-start.47) | collective-permute-done | bytes 245792 | tf_op jit(solution)/shard_map/ppermute | solution.py:43
  209.2 1.6 collective-permute-start.52
  210.8 2.5 %collective-permute-done.53.refs_2_ = bf16[384,1024]{1,0:T(8,128)(2,1)S(1)} collective-permute-done((bf16[384,1024]{1,0:T(8,128)(2,1)S(1)}, bf16[384,1024]{1,0:T(8,128)(2,1)S(1)}, u32[]{:S(2)}, u32[]{:S(2)}) %collective-permute-start.53) | collective-permute-done | bytes 786464 | tf_op jit(solution)/shard_map/ppermute | solution.py:43
  213.3 3.2 %up_finish_up.1 = (f32[768,1536]{1,0:T(8,128)}, f32[384,768]{1,0:T(8,128)}, f32[8,128]{1,0:T(8,128)S(1)}) custom-call(s32[9]{0:T(128)S(1)} %concatenate.22.refs_0_, bf16[384,1024]{1,0:T(8,128)(2,1)S(1)} %get-tuple-element.203.refs_1_, bf16[384,1024]{1,0:T(8,128)(2,1)S(1)} %collective-permute-done.53.refs_2_, ...), custom_call_target="tpu_custom_call" | custom-call | flops 6899999744 | bytes 1 | tf_op jit(solution)/shard_map/up_finish_up/pallas_call | solution.py:125
  217.0 1.6 collective-permute-done.51.refs_2_
  218.6 2.4 %heads_finish_heads.1 = (f32[768,384]{1,0:T(8,128)}, f32[768,384]{1,0:T(8,128)}, f32[768,384]{1,0:T(8,128)}) custom-call(s32[9]{0:T(128)S(1)} %concatenate.22.refs_0_, bf16[384,640]{1,0:T(8,128)(2,1)S(1)} %get-tuple-element.201.refs_1_, bf16[384,640]{1,0:T(8,128)(2,1)S(1)} %collective-permute-done.51.refs_2_, ...), custom_call_target="tpu_custom_call" | custom-call | flops 9200000000 | bytes 1 | tf_op jit(solution)/shard_map/heads_finish_heads/pallas_call | solution.py:125
  (205 shorter events, 31.3 us)
Async XLA Ops:
  0.7 18.5 %collective-permute-start.2 = (bf16[768,1536]{1,0:T(8,128)(2,1)}, bf16[768,1536]{1,0:T(8,128)(2,1)S(1)}, u32[]{:S(2)}, u32[]{:S(2)}) collective-permute-start(bf16[768,1536]{1,0:T(8,128)(2,1)} %refs_4_.5), channel_id=1, source_target_pairs={{0,1},{1,0},{2,3},{3,2},{4,5},{5,4},{6,7},{7,6},{8,9},{9,8},{10,11... | collective-permute-start | bytes 7077896 | tf_op jit(solution)/shard_map/ppermute | solution.py:43
  1.2 18.0 %collective-permute-start.3 = (bf16[1536,768]{1,0:T(8,128)(2,1)}, bf16[1536,768]{1,0:T(8,128)(2,1)}, u32[]{:S(2)}, u32[]{:S(2)}) collective-permute-start(bf16[1536,768]{1,0:T(8,128)(2,1)} %refs_2_.9), channel_id=1, source_target_pairs={{0,1},{1,0},{2,3},{3,2},{4,5},{5,4},{6,7},{7,6},{8,9},{9,8},{10,11... | collective-permute-start | bytes 7077896 | tf_op jit(solution)/shard_map/ppermute | solution.py:43
  1.4 10.5 %copy-start.44 = (s32[8]{0:T(128)S(1)}, s32[8]{0:T(128)}, u32[]{:S(2)}) copy-start(s32[8]{0:T(128)} %param.27) | copy-start | bytes 100
  1.4 10.6 %copy-start.10 = (bf16[1024,768]{1,0:T(8,128)(2,1)S(1)}, bf16[1024,768]{1,0:T(8,128)(2,1)}, u32[]{:S(2)}) copy-start(bf16[1024,768]{1,0:T(8,128)(2,1)} %refs_1_.5) | copy-start | bytes 4718596
  1.4 10.6 %copy-start.12 = (bf16[768,384]{1,0:T(8,128)(2,1)S(1)}, bf16[768,384]{1,0:T(8,128)(2,1)}, u32[]{:S(2)}) copy-start(bf16[768,384]{1,0:T(8,128)(2,1)} %refs_9_.5) | copy-start | bytes 1769476
  1.5 10.6 %copy-start.13 = (bf16[768,384]{1,0:T(8,128)(2,1)S(1)}, bf16[768,384]{1,0:T(8,128)(2,1)}, u32[]{:S(2)}) copy-start(bf16[768,384]{1,0:T(8,128)(2,1)} %refs_10_.3) | copy-start | bytes 1769476
  1.5 10.6 %copy-start.15 = (bf16[768,384]{1,0:T(8,128)(2,1)S(1)}, bf16[768,384]{1,0:T(8,128)(2,1)}, u32[]{:S(2)}) copy-start(bf16[768,384]{1,0:T(8,128)(2,1)} %refs_11_.3) | copy-start | bytes 1769476
  1.5 10.6 %copy-start.21 = (s32[2,512]{1,0:T(2,128)S(1)}, s32[2,512]{1,0:T(2,128)}, u32[]{:S(2)}) copy-start(s32[2,512]{1,0:T(2,128)} %refs_7_.3) | copy-start | bytes 12292
  1.5 10.6 %copy-start.22 = (s32[2,512]{1,0:T(2,128)S(1)}, s32[2,512]{1,0:T(2,128)}, u32[]{:S(2)}) copy-start(s32[2,512]{1,0:T(2,128)} %refs_8_.4) | copy-start | bytes 12292
  1.5 10.6 %copy-start.23 = (bf16[384]{0:T(512)(128)(2,1)S(1)}, bf16[384]{0:T(512)(128)(2,1)}, u32[]{:S(2)}) copy-start(bf16[384]{0:T(512)(128)(2,1)} %refs_5_.3) | copy-start | bytes 2308
  1.5 10.6 %copy-start.24 = (bf16[384]{0:T(512)(128)(2,1)S(1)}, bf16[384]{0:T(512)(128)(2,1)}, u32[]{:S(2)}) copy-start(bf16[384]{0:T(512)(128)(2,1)} %refs_6_.3) | copy-start | bytes 2308
  10.9 8.3 %collective-permute-start = (bf16[384,512]{1,0:T(8,128)(2,1)}, bf16[384,512]{1,0:T(8,128)(2,1)}, u32[]{:S(2)}, u32[]{:S(2)}) collective-permute-start(bf16[384,512]{1,0:T(8,128)(2,1)} %get-tuple-element.115.refs_8_.refs_5_), channel_id=1, source_target_pairs={{0,1},{1,0},{2,3},{3,2},{4,5},{5,4},{6,7},{7,6},{8,9},{9,8},{10,11... | collective-permute-start | bytes 1179656 | tf_op jit(solution)/shard_map/ppermute | solution.py:43
  11.4 7.8 %collective-permute-start.1 = (bf16[384,768]{1,0:T(8,128)(2,1)}, bf16[384,768]{1,0:T(8,128)(2,1)}, u32[]{:S(2)}, u32[]{:S(2)}) collective-permute-start(bf16[384,768]{1,0:T(8,128)(2,1)} %refs_2_.11), channel_id=1, source_target_pairs={{0,1},{1,0},{2,3},{3,2},{4,5},{5,4},{6,7},{7,6},{8,9},{9,8},{10,11... | collective-permute-start | bytes 1769480 | tf_op jit(solution)/shard_map/ppermute | solution.py:43
  11.5 7.7 %collective-permute-start.4 = (bf16[1,1536]{1,0:T(2,128)(2,1)S(1)}, bf16[1,1536]{1,0:T(2,128)(2,1)S(1)}, u32[]{:S(2)}, u32[]{:S(2)}) collective-permute-start(bf16[1,1536]{1,0:T(2,128)(2,1)S(1)} %convert_element_type.23), channel_id=1, source_target_pairs={{0,1},{1,0},{2,3},{3,2},{4,5},{5,4},{6,7},{7,6},{8,9},{9,8},{10,11... | collective-permute-start | bytes 9224 | tf_op jit(solution)/shard_map/ppermute | solution.py:43
  32.5 27.8 %collective-permute-start.13 = (bf16[512,1536]{1,0:T(8,128)(2,1)}, bf16[512,1536]{1,0:T(8,128)(2,1)}, u32[]{:S(2)}, u32[]{:S(2)}) collective-permute-start(bf16[512,1536]{1,0:T(8,128)(2,1)} %get-tuple-element.125), channel_id=1, source_target_pairs={{0,1},{1,0},{2,3},{3,2},{4,5},{5,4},{6,7},{7,6},{8,9},{9,8},{10,11... | collective-permute-start | bytes 4718600 | tf_op jit(solution)/shard_map/ppermute | solution.py:43
  32.6 4.7 %collective-permute-start.5 = (bf16[8,896]{1,0:T(8,128)(2,1)S(1)}, bf16[8,896]{1,0:T(8,128)(2,1)S(1)}, u32[]{:S(2)}, u32[]{:S(2)}) collective-permute-start(bf16[8,896]{1,0:T(8,128)(2,1)S(1)} %pad_maximum_fusion), channel_id=1, source_target_pairs={{0,2},{2,0},{4,6},{6,4},{8,10},{10,8},{12,14},{14,12},{16,18},{18,... | collective-permute-start | bytes 43016 | tf_op jit(solution)/shard_map/ppermute | solution.py:43
  35.6 3.7 %collective-permute-start.6 = (bf16[8,896]{1,0:T(8,128)(2,1)S(1)}, bf16[8,896]{1,0:T(8,128)(2,1)S(1)}, u32[]{:S(2)}, u32[]{:S(2)}) collective-permute-start(bf16[8,896]{1,0:T(8,128)(2,1)S(1)} %pad_maximum_fusion), channel_id=1, source_target_pairs={{0,4},{2,6},{4,0},{6,2},{8,12},{10,14},{12,8},{14,10},{16,20},{18,... | collective-permute-start | bytes 43016 | tf_op jit(solution)/shard_map/ppermute | solution.py:43
  37.1 4.6 %collective-permute-start.7 = (bf16[8,896]{1,0:T(8,128)(2,1)S(1)}, bf16[8,896]{1,0:T(8,128)(2,1)S(1)}, u32[]{:S(2)}, u32[]{:S(2)}) collective-permute-start(bf16[8,896]{1,0:T(8,128)(2,1)S(1)} %pad_maximum_fusion), channel_id=1, source_target_pairs={{0,6},{2,4},{4,2},{6,0},{8,14},{10,12},{12,10},{14,8},{16,22},{18,... | collective-permute-start | bytes 43016 | tf_op jit(solution)/shard_map/ppermute | solution.py:43
  41.8 6.1 %collective-permute-start.10 = (bf16[32,896]{1,0:T(8,128)(2,1)S(1)}, bf16[32,896]{1,0:T(8,128)(2,1)S(1)}, u32[]{:S(2)}, u32[]{:S(2)}) collective-permute-start(bf16[32,896]{1,0:T(8,128)(2,1)S(1)} %concatenate.27), channel_id=1, source_target_pairs={{0,24},{2,26},{4,28},{6,30},{8,16},{10,18},{12,20},{14,22},{16,8},... | collective-permute-start | bytes 172040 | tf_op jit(solution)/shard_map/ppermute | solution.py:43
  45.5 4.2 %collective-permute-start.8 = (bf16[32,896]{1,0:T(8,128)(2,1)S(1)}, bf16[32,896]{1,0:T(8,128)(2,1)S(1)}, u32[]{:S(2)}, u32[]{:S(2)}) collective-permute-start(bf16[32,896]{1,0:T(8,128)(2,1)S(1)} %concatenate.27), channel_id=1, source_target_pairs={{0,8},{2,10},{4,12},{6,14},{8,0},{10,2},{12,4},{14,6},{16,24},{18,... | collective-permute-start | bytes 172040 | tf_op jit(solution)/shard_map/ppermute | solution.py:43
  45.5 5.1 %collective-permute-start.9 = (bf16[32,896]{1,0:T(8,128)(2,1)S(1)}, bf16[32,896]{1,0:T(8,128)(2,1)S(1)}, u32[]{:S(2)}, u32[]{:S(2)}) collective-permute-start(bf16[32,896]{1,0:T(8,128)(2,1)S(1)} %concatenate.27), channel_id=1, source_target_pairs={{0,16},{2,18},{4,20},{6,22},{8,24},{10,26},{12,28},{14,30},{16,0},... | collective-permute-start | bytes 172040 | tf_op jit(solution)/shard_map/ppermute | solution.py:43
  50.7 1.6 collective-permute-start.11
  55.8 4.4 %collective-permute-start.12 = (bf16[512,768]{1,0:T(8,128)(2,1)S(1)}, bf16[512,768]{1,0:T(8,128)(2,1)S(1)}, u32[]{:S(2)}, u32[]{:S(2)}) collective-permute-start(bf16[512,768]{1,0:T(8,128)(2,1)S(1)} %get-tuple-element.121.refs_1_), channel_id=1, source_target_pairs={{0,1},{1,0},{2,3},{3,2},{4,5},{5,4},{6,7},{7,6},{8,9},{9,8},{10,11... | collective-permute-start | bytes 2359304 | tf_op jit(solution)/shard_map/ppermute | solution.py:43
  59.7 12.6 %collective-permute-start.16 = (bf16[512,1536]{1,0:T(8,128)(2,1)S(1)}, bf16[512,1536]{1,0:T(8,128)(2,1)S(1)}, u32[]{:S(2)}, u32[]{:S(2)}) collective-permute-start(bf16[512,1536]{1,0:T(8,128)(2,1)S(1)} %unit_back_far.1.refs_5_.refs_1_), channel_id=1, source_target_pairs={{0,1},{1,0},{2,3},{3,2},{4,5},{5,4},{6,7},{7,6},{8,9},{9,8},{10,11... | collective-permute-start | bytes 4718600 | tf_op jit(solution)/shard_map/ppermute | solution.py:43
  60.1 12.1 %collective-permute-start.17 = (bf16[512,768]{1,0:T(8,128)(2,1)S(1)}, bf16[512,768]{1,0:T(8,128)(2,1)S(1)}, u32[]{:S(2)}, u32[]{:S(2)}) collective-permute-start(bf16[512,768]{1,0:T(8,128)(2,1)S(1)} %copy-done.6), channel_id=1, source_target_pairs={{0,1},{1,0},{2,3},{3,2},{4,5},{5,4},{6,7},{7,6},{8,9},{9,8},{10,11... | collective-permute-start | bytes 2359304 | tf_op jit(solution)/shard_map/ppermute | solution.py:43
  70.7 2.4 %collective-permute-start.18 = (bf16[512,768]{1,0:T(8,128)(2,1)S(1)}, bf16[512,768]{1,0:T(8,128)(2,1)S(1)}, u32[]{:S(2)}, u32[]{:S(2)}) collective-permute-start(bf16[512,768]{1,0:T(8,128)(2,1)S(1)} %get-tuple-element.132.refs_5_.refs_1_), channel_id=1, source_target_pairs={{0,1},{1,0},{2,3},{3,2},{4,5},{5,4},{6,7},{7,6},{8,9},{9,8},{10,11... | collective-permute-start | bytes 2359304 | tf_op jit(solution)/shard_map/ppermute | solution.py:43
  71.2 15.4 %collective-permute-start.14 = (bf16[384,768]{1,0:T(8,128)(2,1)S(1)}, bf16[384,768]{1,0:T(8,128)(2,1)S(1)}, u32[]{:S(2)}, u32[]{:S(2)}) collective-permute-start(bf16[384,768]{1,0:T(8,128)(2,1)S(1)} %get-tuple-element.139), channel_id=1, source_target_pairs={{0,2},{2,0},{4,6},{6,4},{8,10},{10,8},{12,14},{14,12},{16,18},{18,... | collective-permute-start | bytes 1769480 | tf_op jit(solution)/shard_map/ppermute | solution.py:43
  71.7 15.1 %collective-permute-start.15 = (bf16[384,768]{1,0:T(8,128)(2,1)S(1)}, bf16[384,768]{1,0:T(8,128)(2,1)S(1)}, u32[]{:S(2)}, u32[]{:S(2)}) collective-permute-start(bf16[384,768]{1,0:T(8,128)(2,1)S(1)} %get-tuple-element.140), channel_id=1, source_target_pairs={{0,4},{2,6},{4,0},{6,2},{8,12},{10,14},{12,8},{14,10},{16,20},{18,... | collective-permute-start | bytes 1769480 | tf_op jit(solution)/shard_map/ppermute | solution.py:43
  72.2 46.4 %collective-permute-start.22 = (f32[8,768]{1,0:T(8,128)S(1)}, f32[8,768]{1,0:T(8,128)S(1)}, u32[]{:S(2)}, u32[]{:S(2)}) collective-permute-start(f32[8,768]{1,0:T(8,128)S(1)} %get-tuple-element.142.refs_9_.refs_8_), channel_id=1, source_target_pairs={{0,1},{1,0},{2,3},{3,2},{4,5},{5,4},{6,7},{7,6},{8,9},{9,8},{10,11... | collective-permute-start | bytes 73736 | tf_op jit(solution)/shard_map/ppermute | solution.py:43
  87.7 10.9 %collective-permute-start.19 = (bf16[192,768]{1,0:T(8,128)(2,1)S(1)}, bf16[192,768]{1,0:T(8,128)(2,1)S(1)}, u32[]{:S(2)}, u32[]{:S(2)}) collective-permute-start(bf16[192,768]{1,0:T(8,128)(2,1)S(1)} %get-tuple-element.152), channel_id=1, source_target_pairs={{0,4},{2,6},{4,0},{6,2},{8,12},{10,14},{12,8},{14,10},{16,20},{18,... | collective-permute-start | bytes 884744 | tf_op jit(solution)/shard_map/ppermute | solution.py:43
  88.3 10.4 %collective-permute-start.20 = (bf16[192,768]{1,0:T(8,128)(2,1)S(1)}, bf16[192,768]{1,0:T(8,128)(2,1)S(1)}, u32[]{:S(2)}, u32[]{:S(2)}) collective-permute-start(bf16[192,768]{1,0:T(8,128)(2,1)S(1)} %get-tuple-element.153), channel_id=1, source_target_pairs={{0,2},{2,0},{4,6},{6,4},{8,10},{10,8},{12,14},{14,12},{16,18},{18,... | collective-permute-start | bytes 884744 | tf_op jit(solution)/shard_map/ppermute | solution.py:43
  89.7 23.1 %collective-permute-start.24 = (bf16[384,1024]{1,0:T(8,128)(2,1)S(1)}, bf16[384,1024]{1,0:T(8,128)(2,1)S(1)}, u32[]{:S(2)}, u32[]{:S(2)}) collective-permute-start(bf16[384,1024]{1,0:T(8,128)(2,1)S(1)} %get-tuple-element.164), channel_id=1, source_target_pairs={{0,2},{2,0},{4,6},{6,4},{8,10},{10,8},{12,14},{14,12},{16,18},{18,... | collective-permute-start | bytes 2359304 | tf_op jit(solution)/shard_map/ppermute | solution.py:43
  90.3 20.2 %collective-permute-start.25 = (bf16[384,896]{1,0:T(8,128)(2,1)S(1)}, bf16[384,896]{1,0:T(8,128)(2,1)S(1)}, u32[]{:S(2)}, u32[]{:S(2)}) collective-permute-start(bf16[384,896]{1,0:T(8,128)(2,1)S(1)} %get-tuple-element.166), channel_id=1, source_target_pairs={{0,4},{2,6},{4,0},{6,2},{8,12},{10,14},{12,8},{14,10},{16,20},{18,... | collective-permute-start | bytes 2064392 | tf_op jit(solution)/shard_map/ppermute | solution.py:43
  99.4 14.3 %collective-permute-start.23 = (bf16[96,1536]{1,0:T(8,128)(2,1)S(1)}, bf16[96,1536]{1,0:T(8,128)(2,1)S(1)}, u32[]{:S(2)}, u32[]{:S(2)}) collective-permute-start(bf16[96,1536]{1,0:T(8,128)(2,1)S(1)} %get-tuple-element.162), channel_id=1, source_target_pairs={{0,8},{2,10},{4,12},{6,14},{8,0},{10,2},{12,4},{14,6},{16,24},{18,... | collective-permute-start | bytes 884744 | tf_op jit(solution)/shard_map/ppermute | solution.py:43
  108.5 15.7 %collective-permute-start.21 = (bf16[512,768]{1,0:T(8,128)(2,1)S(1)}, bf16[512,768]{1,0:T(8,128)(2,1)S(1)}, u32[]{:S(2)}, u32[]{:S(2)}) collective-permute-start(bf16[512,768]{1,0:T(8,128)(2,1)S(1)} %get-tuple-element.155.refs_5_), channel_id=1, source_target_pairs={{0,1},{1,0},{2,3},{3,2},{4,5},{5,4},{6,7},{7,6},{8,9},{9,8},{10,11... | collective-permute-start | bytes 2359304 | tf_op jit(solution)/shard_map/ppermute | solution.py:43
  114.3 8.3 %collective-permute-start.30 = (bf16[48,1536]{1,0:T(8,128)(2,1)S(1)}, bf16[48,1536]{1,0:T(8,128)(2,1)S(1)}, u32[]{:S(2)}, u32[]{:S(2)}) collective-permute-start(bf16[48,1536]{1,0:T(8,128)(2,1)S(1)} %get-tuple-element.176), channel_id=1, source_target_pairs={{0,16},{2,18},{4,20},{6,22},{8,24},{10,26},{12,28},{14,30},{16,0},... | collective-permute-start | bytes 442376 | tf_op jit(solution)/shard_map/ppermute | solution.py:43
  115.6 11.7 %collective-permute-start.28 = (bf16[192,1024]{1,0:T(8,128)(2,1)S(1)}, bf16[192,1024]{1,0:T(8,128)(2,1)S(1)}, u32[]{:S(2)}, u32[]{:S(2)}) collective-permute-start(bf16[192,1024]{1,0:T(8,128)(2,1)S(1)} %get-tuple-element.174), channel_id=1, source_target_pairs={{0,4},{2,6},{4,0},{6,2},{8,12},{10,14},{12,8},{14,10},{16,20},{18,... | collective-permute-start | bytes 1179656 | tf_op jit(solution)/shard_map/ppermute | solution.py:43
  117.2 10.1 %collective-permute-start.29 = (bf16[192,896]{1,0:T(8,128)(2,1)S(1)}, bf16[192,896]{1,0:T(8,128)(2,1)S(1)}, u32[]{:S(2)}, u32[]{:S(2)}) collective-permute-start(bf16[192,896]{1,0:T(8,128)(2,1)S(1)} %get-tuple-element.175), channel_id=1, source_target_pairs={{0,2},{2,0},{4,6},{6,4},{8,10},{10,8},{12,14},{14,12},{16,18},{18,... | collective-permute-start | bytes 1032200 | tf_op jit(solution)/shard_map/ppermute | solution.py:43
  122.0 13.4 %collective-permute-start.26 = (bf16[400,640]{1,0:T(8,128)(2,1)S(1)}, bf16[400,640]{1,0:T(8,128)(2,1)S(1)}, u32[]{:S(2)}, u32[]{:S(2)}) collective-permute-start(bf16[400,640]{1,0:T(8,128)(2,1)S(1)} %get-tuple-element.170), channel_id=1, source_target_pairs={{0,2},{2,0},{4,6},{6,4},{8,10},{10,8},{12,14},{14,12},{16,18},{18,... | collective-permute-start | bytes 1536008 | tf_op jit(solution)/shard_map/ppermute | solution.py:43
  122.7 10.0 %collective-permute-start.27 = (bf16[384,512]{1,0:T(8,128)(2,1)S(1)}, bf16[384,512]{1,0:T(8,128)(2,1)S(1)}, u32[]{:S(2)}, u32[]{:S(2)}) collective-permute-start(bf16[384,512]{1,0:T(8,128)(2,1)S(1)} %get-tuple-element.172), channel_id=1, source_target_pairs={{0,4},{2,6},{4,0},{6,2},{8,12},{10,14},{12,8},{14,10},{16,20},{18,... | collective-permute-start | bytes 1179656 | tf_op jit(solution)/shard_map/ppermute | solution.py:43
  124.2 13.9 %collective-permute-start.34 = (bf16[48,1536]{1,0:T(8,128)(2,1)S(1)}, bf16[48,1536]{1,0:T(8,128)(2,1)S(1)}, u32[]{:S(2)}, u32[]{:S(2)}) collective-permute-start(bf16[48,1536]{1,0:T(8,128)(2,1)S(1)} %down_add_last.1.refs_5_.refs_1_), channel_id=1, source_target_pairs={{0,16},{2,18},{4,20},{6,22},{8,24},{10,26},{12,28},{14,30},{16,0},... | collective-permute-start | bytes 442376 | tf_op jit(solution)/shard_map/ppermute | solution.py:43
  128.0 11.8 %collective-permute-start.33 = (bf16[96,1920]{1,0:T(8,128)(2,1)S(1)}, bf16[96,1920]{1,0:T(8,128)(2,1)S(1)}, u32[]{:S(2)}, u32[]{:S(2)}) collective-permute-start(bf16[96,1920]{1,0:T(8,128)(2,1)S(1)} %get-tuple-element.182), channel_id=1, source_target_pairs={{0,8},{2,10},{4,12},{6,14},{8,0},{10,2},{12,4},{14,6},{16,24},{18,... | collective-permute-start | bytes 1105928 | tf_op jit(solution)/shard_map/ppermute | solution.py:43
  136.2 7.0 %collective-permute-start.31 = (bf16[208,640]{1,0:T(8,128)(2,1)S(1)}, bf16[208,640]{1,0:T(8,128)(2,1)S(1)}, u32[]{:S(2)}, u32[]{:S(2)}) collective-permute-start(bf16[208,640]{1,0:T(8,128)(2,1)S(1)} %get-tuple-element.179), channel_id=1, source_target_pairs={{0,4},{2,6},{4,0},{6,2},{8,12},{10,14},{12,8},{14,10},{16,20},{18,... | collective-permute-start | bytes 798728 | tf_op jit(solution)/shard_map/ppermute | solution.py:43
  136.7 6.5 %collective-permute-start.32 = (bf16[192,512]{1,0:T(8,128)(2,1)S(1)}, bf16[192,512]{1,0:T(8,128)(2,1)S(1)}, u32[]{:S(2)}, u32[]{:S(2)}) collective-permute-start(bf16[192,512]{1,0:T(8,128)(2,1)S(1)} %get-tuple-element.181), channel_id=1, source_target_pairs={{0,2},{2,0},{4,6},{6,4},{8,10},{10,8},{12,14},{14,12},{16,18},{18,... | collective-permute-start | bytes 589832 | tf_op jit(solution)/shard_map/ppermute | solution.py:43
  138.7 11.7 %collective-permute-start.37 = (bf16[96,1536]{1,0:T(8,128)(2,1)S(1)}, bf16[96,1536]{1,0:T(8,128)(2,1)S(1)}, u32[]{:S(2)}, u32[]{:S(2)}) collective-permute-start(bf16[96,1536]{1,0:T(8,128)(2,1)S(1)} %down_join_pieces.1.refs_3_.refs_1_), channel_id=1, source_target_pairs={{0,8},{2,10},{4,12},{6,14},{8,0},{10,2},{12,4},{14,6},{16,24},{18,... | collective-permute-start | bytes 884744 | tf_op jit(solution)/shard_map/ppermute | solution.py:43
  140.5 15.1 %collective-permute-start.36 = (bf16[48,1920]{1,0:T(8,128)(2,1)S(1)}, bf16[48,1920]{1,0:T(8,128)(2,1)S(1)}, u32[]{:S(2)}, u32[]{:S(2)}) collective-permute-start(bf16[48,1920]{1,0:T(8,128)(2,1)S(1)} %get-tuple-element.186), channel_id=1, source_target_pairs={{0,16},{2,18},{4,20},{6,22},{8,24},{10,26},{12,28},{14,30},{16,0},... | collective-permute-start | bytes 552968 | tf_op jit(solution)/shard_map/ppermute | solution.py:43
  143.9 12.5 %collective-permute-start.35 = (bf16[112,1152]{1,0:T(8,128)(2,1)S(1)}, bf16[112,1152]{1,0:T(8,128)(2,1)S(1)}, u32[]{:S(2)}, u32[]{:S(2)}) collective-permute-start(bf16[112,1152]{1,0:T(8,128)(2,1)S(1)} %get-tuple-element.185), channel_id=1, source_target_pairs={{0,8},{2,10},{4,12},{6,14},{8,0},{10,2},{12,4},{14,6},{16,24},{18,... | collective-permute-start | bytes 774152 | tf_op jit(solution)/shard_map/ppermute | solution.py:43
  151.0 16.0 %collective-permute-start.39 = (bf16[192,768]{1,0:T(8,128)(2,1)S(1)}, bf16[192,768]{1,0:T(8,128)(2,1)S(1)}, u32[]{:S(2)}, u32[]{:S(2)}) collective-permute-start(bf16[192,768]{1,0:T(8,128)(2,1)S(1)} %get-tuple-element.190.refs_1_), channel_id=1, source_target_pairs={{0,4},{2,6},{4,0},{6,2},{8,12},{10,14},{12,8},{14,10},{16,20},{18,... | collective-permute-start | bytes 884744 | tf_op jit(solution)/shard_map/ppermute | solution.py:43
  153.4 13.6 %collective-permute-start.40 = (bf16[192,768]{1,0:T(8,128)(2,1)S(1)}, bf16[192,768]{1,0:T(8,128)(2,1)S(1)}, u32[]{:S(2)}, u32[]{:S(2)}) collective-permute-start(bf16[192,768]{1,0:T(8,128)(2,1)S(1)} %get-tuple-element.187.refs_3_), channel_id=1, source_target_pairs={{0,2},{2,0},{4,6},{6,4},{8,10},{10,8},{12,14},{14,12},{16,18},{18,... | collective-permute-start | bytes 884744 | tf_op jit(solution)/shard_map/ppermute | solution.py:43
  156.2 10.1 %collective-permute-start.41 = (bf16[48,1920]{1,0:T(8,128)(2,1)S(1)}, bf16[48,1920]{1,0:T(8,128)(2,1)S(1)}, u32[]{:S(2)}, u32[]{:S(2)}) collective-permute-start(bf16[48,1920]{1,0:T(8,128)(2,1)S(1)} %up_add_last.1.refs_3_.refs_1_), channel_id=1, source_target_pairs={{0,16},{2,18},{4,20},{6,22},{8,24},{10,26},{12,28},{14,30},{16,0},... | collective-permute-start | bytes 552968 | tf_op jit(solution)/shard_map/ppermute | solution.py:43
  157.0 12.8 %collective-permute-start.38 = (bf16[64,1152]{1,0:T(8,128)(2,1)S(1)}, bf16[64,1152]{1,0:T(8,128)(2,1)S(1)}, u32[]{:S(2)}, u32[]{:S(2)}) collective-permute-start(bf16[64,1152]{1,0:T(8,128)(2,1)S(1)} %get-tuple-element.189), channel_id=1, source_target_pairs={{0,16},{2,18},{4,20},{6,22},{8,24},{10,26},{12,28},{14,30},{16,0},... | collective-permute-start | bytes 442376 | tf_op jit(solution)/shard_map/ppermute | solution.py:43
  166.9 7.6 %collective-permute-start.43 = (bf16[96,1920]{1,0:T(8,128)(2,1)S(1)}, bf16[96,1920]{1,0:T(8,128)(2,1)S(1)}, u32[]{:S(2)}, u32[]{:S(2)}) collective-permute-start(bf16[96,1920]{1,0:T(8,128)(2,1)S(1)} %up_join_pieces.1.refs_5_.refs_1_), channel_id=1, source_target_pairs={{0,8},{2,10},{4,12},{6,14},{8,0},{10,2},{12,4},{14,6},{16,24},{18,... | collective-permute-start | bytes 1105928 | tf_op jit(solution)/shard_map/ppermute | solution.py:43
  167.6 25.2 %collective-permute-start.49 = (bf16[384,768]{1,0:T(8,128)(2,1)S(1)}, bf16[384,768]{1,0:T(8,128)(2,1)S(1)}, u32[]{:S(2)}, u32[]{:S(2)}) collective-permute-start(bf16[384,768]{1,0:T(8,128)(2,1)S(1)} %get-tuple-element.199.refs_1_), channel_id=1, source_target_pairs={{0,2},{2,0},{4,6},{6,4},{8,10},{10,8},{12,14},{14,12},{16,18},{18,... | collective-permute-start | bytes 1769480 | tf_op jit(solution)/shard_map/ppermute | solution.py:43
  167.7 26.7 %collective-permute-start.50 = (bf16[384,768]{1,0:T(8,128)(2,1)S(1)}, bf16[384,768]{1,0:T(8,128)(2,1)S(1)}, u32[]{:S(2)}, u32[]{:S(2)}) collective-permute-start(bf16[384,768]{1,0:T(8,128)(2,1)S(1)} %get-tuple-element.191.refs_3_), channel_id=1, source_target_pairs={{0,4},{2,6},{4,0},{6,2},{8,12},{10,14},{12,8},{14,10},{16,20},{18,... | collective-permute-start | bytes 1769480 | tf_op jit(solution)/shard_map/ppermute | solution.py:43
  170.3 7.1 %collective-permute-start.42 = (bf16[48,1152]{1,0:T(8,128)(2,1)S(1)}, bf16[48,1152]{1,0:T(8,128)(2,1)S(1)}, u32[]{:S(2)}, u32[]{:S(2)}) collective-permute-start(bf16[48,1152]{1,0:T(8,128)(2,1)S(1)} %get-tuple-element.192.refs_1_), channel_id=1, source_target_pairs={{0,16},{2,18},{4,20},{6,22},{8,24},{10,26},{12,28},{14,30},{16,0},... | collective-permute-start | bytes 331784 | tf_op jit(solution)/shard_map/ppermute | solution.py:43
  175.8 11.3 %collective-permute-start.45 = (bf16[192,1024]{1,0:T(8,128)(2,1)S(1)}, bf16[192,1024]{1,0:T(8,128)(2,1)S(1)}, u32[]{:S(2)}, u32[]{:S(2)}) collective-permute-start(bf16[192,1024]{1,0:T(8,128)(2,1)S(1)} %get-tuple-element.195.refs_1_), channel_id=1, source_target_pairs={{0,4},{2,6},{4,0},{6,2},{8,12},{10,14},{12,8},{14,10},{16,20},{18,... | collective-permute-start | bytes 1179656 | tf_op jit(solution)/shard_map/ppermute | solution.py:43
  175.8 9.2 %collective-permute-start.46 = (bf16[192,896]{1,0:T(8,128)(2,1)}, bf16[192,896]{1,0:T(8,128)(2,1)}, u32[]{:S(2)}, u32[]{:S(2)}) collective-permute-start(bf16[192,896]{1,0:T(8,128)(2,1)} %get-tuple-element.194.refs_3_), channel_id=1, source_target_pairs={{0,2},{2,0},{4,6},{6,4},{8,10},{10,8},{12,14},{14,12},{16,18},{18,... | collective-permute-start | bytes 1032200 | tf_op jit(solution)/shard_map/ppermute | solution.py:43
  179.6 10.4 %collective-permute-start.44 = (bf16[96,1152]{1,0:T(8,128)(2,1)S(1)}, bf16[96,1152]{1,0:T(8,128)(2,1)}, u32[]{:S(2)}, u32[]{:S(2)}) collective-permute-start(bf16[96,1152]{1,0:T(8,128)(2,1)S(1)} %heads_join_pieces.1.refs_5_.refs_1_), channel_id=1, source_target_pairs={{0,8},{2,10},{4,12},{6,14},{8,0},{10,2},{12,4},{14,6},{16,24},{18,... | collective-permute-start | bytes 663560 | tf_op jit(solution)/shard_map/ppermute | solution.py:43
  188.3 22.5 %collective-permute-start.54 = (bf16[384,896]{1,0:T(8,128)(2,1)S(1)}, bf16[384,896]{1,0:T(8,128)(2,1)S(1)}, u32[]{:S(2)}, u32[]{:S(2)}) collective-permute-start(bf16[384,896]{1,0:T(8,128)(2,1)S(1)} %get-tuple-element.196.refs_3_), channel_id=1, source_target_pairs={{0,4},{2,6},{4,0},{6,2},{8,12},{10,14},{12,8},{14,10},{16,20},{18,... | collective-permute-start | bytes 2064392 | tf_op jit(solution)/shard_map/ppermute | solution.py:43
  191.9 16.6 %collective-permute-start.47 = (bf16[192,640]{1,0:T(8,128)(2,1)S(1)}, bf16[192,640]{1,0:T(8,128)(2,1)S(1)}, u32[]{:S(2)}, u32[]{:S(2)}) collective-permute-start(bf16[192,640]{1,0:T(8,128)(2,1)S(1)} %get-tuple-element.197.refs_1_), channel_id=1, source_target_pairs={{0,4},{2,6},{4,0},{6,2},{8,12},{10,14},{12,8},{14,10},{16,20},{18,... | collective-permute-start | bytes 737288 | tf_op jit(solution)/shard_map/ppermute | solution.py:43
  192.4 7.2 %collective-permute-start.48 = (bf16[192,512]{1,0:T(8,128)(2,1)S(1)}, bf16[192,512]{1,0:T(8,128)(2,1)S(1)}, u32[]{:S(2)}, u32[]{:S(2)}) collective-permute-start(bf16[192,512]{1,0:T(8,128)(2,1)S(1)} %get-tuple-element.198.refs_5_.refs_3_), channel_id=1, source_target_pairs={{0,2},{2,0},{4,6},{6,4},{8,10},{10,8},{12,14},{14,12},{16,18},{18,... | collective-permute-start | bytes 589832 | tf_op jit(solution)/shard_map/ppermute | solution.py:43
  192.9 20.5 %collective-permute-start.53 = (bf16[384,1024]{1,0:T(8,128)(2,1)S(1)}, bf16[384,1024]{1,0:T(8,128)(2,1)S(1)}, u32[]{:S(2)}, u32[]{:S(2)}) collective-permute-start(bf16[384,1024]{1,0:T(8,128)(2,1)S(1)} %get-tuple-element.203.refs_1_), channel_id=1, source_target_pairs={{0,2},{2,0},{4,6},{6,4},{8,10},{10,8},{12,14},{14,12},{16,18},{18,... | collective-permute-start | bytes 2359304 | tf_op jit(solution)/shard_map/ppermute | solution.py:43
  209.1 9.5 %collective-permute-start.51 = (bf16[384,640]{1,0:T(8,128)(2,1)S(1)}, bf16[384,640]{1,0:T(8,128)(2,1)S(1)}, u32[]{:S(2)}, u32[]{:S(2)}) collective-permute-start(bf16[384,640]{1,0:T(8,128)(2,1)S(1)} %get-tuple-element.201.refs_1_), channel_id=1, source_target_pairs={{0,2},{2,0},{4,6},{6,4},{8,10},{10,8},{12,14},{14,12},{16,18},{18,... | collective-permute-start | bytes 1474568 | tf_op jit(solution)/shard_map/ppermute | solution.py:43
  209.2 7.8 %collective-permute-start.52 = (bf16[384,512]{1,0:T(8,128)(2,1)S(1)}, bf16[384,512]{1,0:T(8,128)(2,1)S(1)}, u32[]{:S(2)}, u32[]{:S(2)}) collective-permute-start(bf16[384,512]{1,0:T(8,128)(2,1)S(1)} %get-tuple-element.202.refs_5_.refs_3_), channel_id=1, source_target_pairs={{0,4},{2,6},{4,0},{6,2},{8,12},{10,14},{12,8},{14,10},{16,20},{18,... | collective-permute-start | bytes 1179656 | tf_op jit(solution)/shard_map/ppermute | solution.py:43
  (36 other events, 159.1 us)
where the time goes:
time: 222 us; the launch traced here: 221 us
  Pallas kernels  91.9 us (41%)
  waiting for transfers between devices  66.3 us (30%)
  starting transfers between devices  51.1 us (23%)
  local copies, waits for them, and re-layouts  8.7 us (4%)
    pallas_call x36, Pallas kernels, call(): pl.pallas_call(body, name=name, out_shape=[jax.ShapeDtypeStruct(*out) if...  91.9 us
    ppermute x55, waiting for transfers between devices, flip_by(): return lax.ppermute(value, axis, [(i, i ^ mask) for i in range(size)])  66.3 us
    ppermute x55, starting transfers between devices, flip_by(): return lax.ppermute(value, axis, [(i, i ^ mask) for i in range(size)])  51.1 us
  transfers between devices with their start and end apart: 55, of which 26 were waited for; matrix products, arithmetic and copies ran while one was open for 3% of the time, Pallas kernels for 34%

commit v1 on v0

--- a/solution.py
+++ b/solution.py
@@ -527,9 +527,10 @@
     step = length // 2
     halves = (pl.ds(0, step), pl.ds(step, step))
     base = info[BT] * length
-    context, output_near, tokens = ready(context, output_near, tokens)
+    context, output_near = ready(context, output_near)
     for at in halves:
         heads = t_dot(context[:, at], output_near[...]) + t_dot(context_in[:, at], output_far[...])
+        (tokens,) = ready(tokens)
         x = tokens[pl.ds(pl.multiple_of(base + at.start, step), step)].astype(f32)
         normed, scale = center(x + (heads + vectors[OB : OB + 1]))
         out = normed * vectors[FG : FG + 1] + vectors[FS : FS + 1]
@@ -750,7 +751,7 @@
             + [((heads_local, length, length), bf16), ((heads_local + -heads_local % 8, length), f32)],
             info, tokens, query_weight, key_weight, value_weight, query_bias, value_bias, segments, validity,
             scratch=[pltpu.VMEM((length, length), f32)],
-            late=(1, 2, 3, 4, 5, 6, 7, 8) if far else (),
+            late=(7, 8, 1, 2, 5, 6, 3, 4) if far else (),
             early=(0, 1, 2, 3, 4, 5),
         )
 

time: 222 us -> 221 us (level)
  transfers between devices with their start and end apart: 55 -> 55, of which waited for: 26 -> 25; matrix products, arithmetic and copies ran while one was open for 3% -> 3% of each run, Pallas kernels for 34% -> 34%
where the time goes in v1:
time: 221 us
  Pallas kernels  91.4 us (41%)
  waiting for transfers between devices  67.4 us (30%)
  starting transfers between devices  50.3 us (23%)
  local copies, waits for them, and re-layouts  8.69 us (4%)
    pallas_call x36, Pallas kernels, call(): pl.pallas_call(body, name=name, out_shape=[jax.ShapeDtypeStruct(*out) if...  91.4 us
    ppermute x55, waiting for transfers between devices, flip_by(): return lax.ppermute(value, axis, [(i, i ^ mask) for i in range(size)])  67.4 us
    ppermute x55, starting transfers between devices, flip_by(): return lax.ppermute(value, axis, [(i, i ^ mask) for i in range(size)])  50.3 us
  transfers between devices with their start and end apart: 55, of which 25 were waited for; matrix products, arithmetic and copies ran while one was open for 3% of the time, Pallas kernels for 34%

profile of v1, /device:TPU:0, one launch (start us, length us, event | category | flops | bytes accessed | tf_op | source)
XLA Modules:
  0.0 221.1 jit_solution(14507933275529034272)
XLA Ops:
  1.5 8.9 %attend_far.1 = (bf16[384,512]{1,0:T(8,128)(2,1)}, bf16[512,384]{1,0:T(8,128)(2,1)}, bf16[512,384]{1,0:T(8,128)(2,1)}, bf16[512,384]{1,0:T(8,128)(2,1)}, bf16[6,512,512]{2,1,0:T(8,128)(2,1)}, /*index=5*/f32[8,512]{1,0:T(8,128)}) custom-call(s32[9]{0:T(128)S(1)} %concatenate.22.refs_0_, bf16[1024,768]{1,0:T(8,128)(2,1)} %refs_1_.5, bf16[768,384]{1,0:T(8,128)(2,1)} %refs_9_.5, ...), custom_call_target="tpu_custom_call" | custom-call | flops 9200000000 | bytes 1 | tf_op jit(solution)/shard_map/attend_far/pallas_call | solution.py:125
  11.7 6.6 %attend_near.1 = (bf16[384,512]{1,0:T(8,128)(2,1)}, bf16[512,384]{1,0:T(8,128)(2,1)}, bf16[512,384]{1,0:T(8,128)(2,1)}, bf16[512,384]{1,0:T(8,128)(2,1)}, bf16[6...) custom-call(s32[9]{0:T(128)S(1)} %concatenate.22.refs_0_, bf16[1024,768]{1,0:T(8,128)(2,1)S(1)} %copy-done.10, ...), custom_call_target="tpu_custom_call" | custom-call | flops 8049999872 | bytes 1 | tf_op jit(solution)/shard_map/attend_near/pallas_call | solution.py:125
  18.8 13.2 %forward.1 = (bf16[512,768]{1,0:T(8,128)(2,1)}, bf16[512,768]{1,0:T(8,128)(2,1)}, f32[512,1]{1,0:T(8,128)}, bf16[512,1536]{1,0:T(8,128)(2,1)}, bf16[512,1536]{1,...) custom-call(s32[9]{0:T(128)S(1)} %concatenate.22.refs_0_, ...), custom_call_target="tpu_custom_call" | custom-call | flops 17250000896 | bytes 1 | tf_op jit(solution)/shard_map/forward/pallas_call | solution.py:125
  32.2 3.0 %collective-permute-start.5 = (bf16[8,896]{1,0:T(8,128)(2,1)S(1)}, bf16[8,896]{1,0:T(8,128)(2,1)S(1)}, u32[]{:S(2)}, u32[]{:S(2)}) collective-permute-start(bf16[8,896]{1,0:T(8,128)(2,1)S(1)} %pad_maximum_fusion), channel_id=1, source_target_pairs={{0,2},{2,0},{4,6},{6,4},{8,10},{10,8},{12,14},{14,12},{16,18},{18,... | collective-permute-start | bytes 43016 | tf_op jit(solution)/shard_map/ppermute | solution.py:43
  35.2 1.5 collective-permute-start.6
  36.9 2.0 collective-permute-done.6
  38.9 2.4 %collective-permute-done.7 = bf16[8,896]{1,0:T(8,128)(2,1)S(1)} collective-permute-done((bf16[8,896]{1,0:T(8,128)(2,1)S(1)}, bf16[8,896]{1,0:T(8,128)(2,1)S(1)}, u32[]{:S(2)}, u32[]{:S(2)}) %collective-permute-start.7) | collective-permute-done | bytes 14368 | tf_op jit(solution)/shard_map/ppermute | solution.py:43
  41.4 3.7 %collective-permute-start.10 = (bf16[32,896]{1,0:T(8,128)(2,1)S(1)}, bf16[32,896]{1,0:T(8,128)(2,1)S(1)}, u32[]{:S(2)}, u32[]{:S(2)}) collective-permute-start(bf16[32,896]{1,0:T(8,128)(2,1)S(1)} %concatenate.27), channel_id=1, source_target_pairs={{0,24},{2,26},{4,28},{6,30},{8,16},{10,18},{12,20},{14,22},{16,8},... | collective-permute-start | bytes 172040 | tf_op jit(solution)/shard_map/ppermute | solution.py:43
  45.8 1.7 collective-permute-done.10
  47.5 1.7 collective-permute-done.8
  50.3 1.5 collective-permute-done.11.refs_2_
  51.8 3.6 %loss_back.1 = (f32[1,8]{1,0:T(1,128)}, f32[8,768]{1,0:T(8,128)}, f32[512,768]{1,0:T(8,128)S(1)}, bf16[512,768]{1,0:T(8,128)(2,1)S(1)}, f32[8,768]{1,0:T(8,128)S(1)}) custom-call(s32[9]{0:T(128)S(1)} %concatenate.22.refs_0_, bf16[128,896]{1,0:T(8,128)(2,1)S(1)} %concatenate.28.refs_1_, bf16[128,896]{1,0:T(8,128)(2,1)S(1)} %collective-permute-done.11.refs_2_, ...), custom_call_target="tpu_custom_call" | custom-call | flops 4600000000 | bytes 1 | tf_op jit(solution)/shard_map/loss_back/pallas_call | solution.py:125
  55.6 3.6 %unit_back_far.1.refs_5_.refs_1_ = bf16[512,1536]{1,0:T(8,128)(2,1)S(1)} custom-call(s32[9]{0:T(128)S(1)} %concatenate.22.refs_0_, bf16[512,768]{1,0:T(8,128)(2,1)S(1)} %get-tuple-element.121.refs_1_, bf16[1536,768]{1,0:T(8,128)(2,1)} %collective-permute-done.3.refs_7_.refs_2_, bf16[512,1536]{1,0:T(8,128)(2,1)S(1)} %copy-done.28), custom_call_target="tpu_custom_call" | custom-call | flops 4600000000 | bytes 1 | tf_op jit(solution)/shard_map/unit_back_far/pallas_call | solution.py:125
  59.9 4.3 %down_gradient.1 = (bf16[384,768]{1,0:T(8,128)(2,1)S(1)}, bf16[384,768]{1,0:T(8,128)(2,1)S(1)}, bf16[384,768]{1,0:T(8,128)(2,1)S(1)}, bf16[384,768]{1,0:T(8,128)(2,1)S(1)}) custom-call(s32[9]{0:T(128)S(1)} %concatenate.22.refs_0_, bf16[512,768]{1,0:T(8,128)(2,1)S(1)} %get-tuple-element.121.refs_1_, bf16[512,1536]{1,0:T(8,128)(2,1)S(1)} %copy-done.27, ...), custom_call_target="tpu_custom_call" | custom-call | flops 3449999872 | bytes 1 | tf_op jit(solution)/shard_map/down_gradient/pallas_call | solution.py:125
  64.2 2.2 unit_back_near.1.refs_3_.refs_10_.refs_1_
  66.4 3.8 %first_back.1 = (f32[512,768]{1,0:T(8,128)S(1)}, bf16[512,768]{1,0:T(8,128)(2,1)S(1)}, f32[8,768]{1,0:T(8,128)S(1)}) custom-call(s32[9]{0:T(128)S(1)} %concatenate.22.refs_0_, bf16[512,1536]{1,0:T(8,128)(2,1)S(1)} %unit_back_far.1.refs_5_.refs_1_, bf16[768,1536]{1,0:T(8,128)(2,1)S(1)} %collective-permute-done.2.refs_6_.refs_2_, ...), custom_call_target="tpu_custom_call" | custom-call | flops 2070000000 | bytes 1 | tf_op jit(solution)/shard_map/first_back/pallas_call | solution.py:125
  72.7 4.4 %up_gradient.1 = (bf16[384,1024]{1,0:T(8,128)(2,1)S(1)}, bf16[384,896]{1,0:T(8,128)(2,1)S(1)}, bf16[384,1024]{1,0:T(8,128)(2,1)S(1)}, bf16[384,896]{1,0:T(8,128)(2,1)S(1)}, f32[8,1536]{1,0:T(8,128)S(1)}) custom-call(s32[9]{0:T(128)S(1)} %concatenate.22.refs_0_, bf16[512,1536]{1,0:T(8,128)(2,1)S(1)} %unit_back_near.1.refs_3_.refs_10_.refs_1_, ...), custom_call_target="tpu_custom_call" | custom-call | flops 184000000 | bytes 1 | tf_op jit(solution)/shard_map/up_gradient/pallas_call | solution.py:125
  77.0 9.1 %collective-permute-done.14.refs_2_ = bf16[384,768]{1,0:T(8,128)(2,1)S(1)} collective-permute-done((bf16[384,768]{1,0:T(8,128)(2,1)S(1)}, bf16[384,768]{1,0:T(8,128)(2,1)S(1)}, u32[]{:S(2)}, u32[]{:S(2)}) %collective-permute-start.14) | collective-permute-done | bytes 589856 | tf_op jit(solution)/shard_map/ppermute | solution.py:43
  87.8 1.5 collective-permute-start.20
  89.8 1.5 collective-permute-start.25
  91.4 6.7 %attend_back_near.1 = (bf16[512,384]{1,0:T(8,128)(2,1)S(1)}, bf16[512,384]{1,0:T(8,128)(2,1)S(1)}, bf16[512,384]{1,0:T(8,128)(2,1)S(1)}, f32[512,768]{1,0:T(8,128)S(1)}) custom-call(s32[9]{0:T(128)S(1)} %concatenate.22.refs_0_, bf16[512,768]{1,0:T(8,128)(2,1)S(1)} %get-tuple-element.132.refs_5_.refs_1_, bf16[384,768]{1,0:T(8,128)(2,1)} %refs_2_.11, ...), custom_call_target="tpu_custom_call" | custom-call | flops 4024999936 | bytes 1 | tf_op jit(solution)/shard_map/attend_back_near/pallas_call | solution.py:125
  98.9 2.1 collective-permute-start.23
  101.1 7.0 %attend_back_far.1 = (bf16[512,384]{1,0:T(8,128)(2,1)S(1)}, bf16[512,384]{1,0:T(8,128)(2,1)S(1)}, bf16[512,384]{1,0:T(8,128)(2,1)S(1)}, bf16[512,768]{1,0:T(8,128)(2,1)S(1)}) custom-call(s32[9]{0:T(128)S(1)} %concatenate.22.refs_0_, bf16[512,768]{1,0:T(8,128)(2,1)S(1)} %collective-permute-done.18.refs_6_.refs_1_, bf16[384,768]{1,0:T(8,128)(2,1)} %refs_2_.11, ...), custom_call_target="tpu_custom_call" | custom-call | flops 4024999936 | bytes 1 | tf_op jit(solution)/shard_map/attend_back_far/pallas_call | solution.py:125
  108.1 1.9 collective-permute-done.25.refs_4_
  110.0 2.3 %collective-permute-done.24.refs_2_ = bf16[384,1024]{1,0:T(8,128)(2,1)S(1)} collective-permute-done((bf16[384,1024]{1,0:T(8,128)(2,1)S(1)}, bf16[384,1024]{1,0:T(8,128)(2,1)S(1)}, u32[]{:S(2)}, u32[]{:S(2)}) %collective-permute-start.24) | collective-permute-done | bytes 786464 | tf_op jit(solution)/shard_map/ppermute | solution.py:43
  113.9 1.3 collective-permute-start.30
  115.2 1.5 collective-permute-start.28
  116.7 1.4 collective-permute-start.29
  118.1 3.4 %head_gradients.1 = (bf16[400,640]{1,0:T(8,128)(2,1)S(1)}, bf16[384,512]{1,0:T(8,128)(2,1)S(1)}, bf16[400,640]{1,0:T(8,128)(2,1)S(1)}, bf16[384,512]{1,0:T(8,128)(2,1)S(1)}) custom-call(s32[9]{0:T(128)S(1)} %concatenate.22.refs_0_, bf16[1024,768]{1,0:T(8,128)(2,1)S(1)} %copy-done.11, bf16[512,384]{1,0:T(8,128)(2,1)S(1)} %get-tuple-element.156.refs_2_, ...), custom_call_target="tpu_custom_call" | custom-call | flops 5750000128 | bytes 1 | tf_op jit(solution)/shard_map/head_gradients/pallas_call | solution.py:125
  122.2 0.9 collective-permute-start.27
  123.8 1.3 collective-permute-start.34
  125.1 1.2 add_convert_fusion
  127.6 1.6 collective-permute-start.33
  129.2 3.0 %collective-permute-done.27.refs_4_ = bf16[384,512]{1,0:T(8,128)(2,1)S(1)} collective-permute-done((bf16[384,512]{1,0:T(8,128)(2,1)S(1)}, bf16[384,512]{1,0:T(8,128)(2,1)S(1)}, u32[]{:S(2)}, u32[]{:S(2)}) %collective-permute-start.27) | collective-permute-done | bytes 393248 | tf_op jit(solution)/shard_map/ppermute | solution.py:43
  132.2 2.8 %collective-permute-done.26.refs_2_ = bf16[400,640]{1,0:T(8,128)(2,1)S(1)} collective-permute-done((bf16[400,640]{1,0:T(8,128)(2,1)S(1)}, bf16[400,640]{1,0:T(8,128)(2,1)S(1)}, u32[]{:S(2)}, u32[]{:S(2)}) %collective-permute-start.26) | collective-permute-done | bytes 512032 | tf_op jit(solution)/shard_map/ppermute | solution.py:43
  136.3 1.4 collective-permute-start.32
  138.3 1.2 collective-permute-start.37
  140.1 2.7 %collective-permute-start.36 = (bf16[48,1920]{1,0:T(8,128)(2,1)S(1)}, bf16[48,1920]{1,0:T(8,128)(2,1)S(1)}, u32[]{:S(2)}, u32[]{:S(2)}) collective-permute-start(bf16[48,1920]{1,0:T(8,128)(2,1)S(1)} %get-tuple-element.186), channel_id=1, source_target_pairs={{0,16},{2,18},{4,20},{6,22},{8,24},{10,26},{12,28},{14,30},{16,0},... | collective-permute-start | bytes 552968 | tf_op jit(solution)/shard_map/ppermute | solution.py:43
  144.1 5.9 %collective-permute-done.37.refs_2_ = bf16[96,1536]{1,0:T(8,128)(2,1)S(1)} collective-permute-done((bf16[96,1536]{1,0:T(8,128)(2,1)S(1)}, bf16[96,1536]{1,0:T(8,128)(2,1)S(1)}, u32[]{:S(2)}, u32[]{:S(2)}) %collective-permute-start.37) | collective-permute-done | bytes 294944 | tf_op jit(solution)/shard_map/ppermute | solution.py:43
  150.6 2.4 %collective-permute-start.39 = (bf16[192,768]{1,0:T(8,128)(2,1)S(1)}, bf16[192,768]{1,0:T(8,128)(2,1)S(1)}, u32[]{:S(2)}, u32[]{:S(2)}) collective-permute-start(bf16[192,768]{1,0:T(8,128)(2,1)S(1)} %get-tuple-element.190.refs_1_), channel_id=1, source_target_pairs={{0,4},{2,6},{4,0},{6,2},{8,12},{10,14},{12,8},{14,10},{16,20},{18,... | collective-permute-start | bytes 884744 | tf_op jit(solution)/shard_map/ppermute | solution.py:43
  153.0 2.0 collective-permute-start.40
  156.5 2.8 %collective-permute-start.38 = (bf16[64,1152]{1,0:T(8,128)(2,1)S(1)}, bf16[64,1152]{1,0:T(8,128)(2,1)S(1)}, u32[]{:S(2)}, u32[]{:S(2)}) collective-permute-start(bf16[64,1152]{1,0:T(8,128)(2,1)S(1)} %get-tuple-element.189), channel_id=1, source_target_pairs={{0,16},{2,18},{4,20},{6,22},{8,24},{10,26},{12,28},{14,30},{16,0},... | collective-permute-start | bytes 442376 | tf_op jit(solution)/shard_map/ppermute | solution.py:43
  159.3 6.3 %collective-permute-done.41.refs_2_ = bf16[48,1920]{1,0:T(8,128)(2,1)S(1)} collective-permute-done((bf16[48,1920]{1,0:T(8,128)(2,1)S(1)}, bf16[48,1920]{1,0:T(8,128)(2,1)S(1)}, u32[]{:S(2)}, u32[]{:S(2)}) %collective-permute-start.41) | collective-permute-done | bytes 184352 | tf_op jit(solution)/shard_map/ppermute | solution.py:43
  166.9 1.1 collective-permute-start.50
  168.0 1.2 collective-permute-done.38.refs_2_
  169.8 1.1 collective-permute-start.42
  171.0 2.8 %collective-permute-done.43.refs_2_ = bf16[96,1920]{1,0:T(8,128)(2,1)S(1)} collective-permute-done((bf16[96,1920]{1,0:T(8,128)(2,1)S(1)}, bf16[96,1920]{1,0:T(8,128)(2,1)S(1)}, u32[]{:S(2)}, u32[]{:S(2)}) %collective-permute-start.43) | collective-permute-done | bytes 368672 | tf_op jit(solution)/shard_map/ppermute | solution.py:43
  173.8 1.3 up_join_eighths.1
  175.1 1.2 collective-permute-start.46
  180.0 1.3 squeeze.23
  184.3 3.3 %collective-permute-done.45.refs_2_ = bf16[192,1024]{1,0:T(8,128)(2,1)S(1)} collective-permute-done((bf16[192,1024]{1,0:T(8,128)(2,1)S(1)}, bf16[192,1024]{1,0:T(8,128)(2,1)S(1)}, u32[]{:S(2)}, u32[]{:S(2)}) %collective-permute-start.45) | collective-permute-done | bytes 393248 | tf_op jit(solution)/shard_map/ppermute | solution.py:43
  187.6 1.2 up_join_quarters.1
  188.9 0.9 copy-done.18
  189.8 1.0 heads_join_eighths.1
  190.8 2.1 collective-permute-start.47
  192.9 1.3 collective-permute-start.48
  194.9 2.8 %down_finish_down.1 = (f32[1536,768]{1,0:T(8,128)}, f32[8,128]{1,0:T(8,128)S(1)}) custom-call(s32[9]{0:T(128)S(1)} %concatenate.22.refs_0_, bf16[384,768]{1,0:T(8,128)(2,1)S(1)} %get-tuple-element.199.refs_1_, bf16[384,768]{1,0:T(8,128)(2,1)S(1)} %collective-permute-done.49.refs_2_, bf16[384,768]{1,0:T(8,128)(2,1)S(1)} %get-tuple-element.191.refs_3_, ...), custom_call_target="tpu_custom_call" | custom-call | flops 6899999744 | bytes 1 | tf_op jit(solution)/shard_map/down_finish_down/pallas_call | solution.py:125
  197.7 1.3 collective-permute-done.48.refs_4_
  199.1 9.9 %collective-permute-done.47.refs_2_ = bf16[192,640]{1,0:T(8,128)(2,1)S(1)} collective-permute-done((bf16[192,640]{1,0:T(8,128)(2,1)S(1)}, bf16[192,640]{1,0:T(8,128)(2,1)S(1)}, u32[]{:S(2)}, u32[]{:S(2)}) %collective-permute-start.47) | collective-permute-done | bytes 245792 | tf_op jit(solution)/shard_map/ppermute | solution.py:43
  209.8 3.0 %collective-permute-done.53.refs_2_ = bf16[384,1024]{1,0:T(8,128)(2,1)S(1)} collective-permute-done((bf16[384,1024]{1,0:T(8,128)(2,1)S(1)}, bf16[384,1024]{1,0:T(8,128)(2,1)S(1)}, u32[]{:S(2)}, u32[]{:S(2)}) %collective-permute-start.53) | collective-permute-done | bytes 786464 | tf_op jit(solution)/shard_map/ppermute | solution.py:43
  212.8 3.2 %up_finish_up.1 = (f32[768,1536]{1,0:T(8,128)}, f32[384,768]{1,0:T(8,128)}, f32[8,128]{1,0:T(8,128)S(1)}) custom-call(s32[9]{0:T(128)S(1)} %concatenate.22.refs_0_, bf16[384,1024]{1,0:T(8,128)(2,1)S(1)} %get-tuple-element.203.refs_1_, bf16[384,1024]{1,0:T(8,128)(2,1)S(1)} %collective-permute-done.53.refs_2_, ...), custom_call_target="tpu_custom_call" | custom-call | flops 6899999744 | bytes 1 | tf_op jit(solution)/shard_map/up_finish_up/pallas_call | solution.py:125
  216.0 1.5 collective-permute-done.52.refs_4_
  217.5 1.0 collective-permute-done.51.refs_2_
  218.5 2.4 %heads_finish_heads.1 = (f32[768,384]{1,0:T(8,128)}, f32[768,384]{1,0:T(8,128)}, f32[768,384]{1,0:T(8,128)}) custom-call(s32[9]{0:T(128)S(1)} %concatenate.22.refs_0_, bf16[384,640]{1,0:T(8,128)(2,1)S(1)} %get-tuple-element.201.refs_1_, bf16[384,640]{1,0:T(8,128)(2,1)S(1)} %collective-permute-done.51.refs_2_, ...), custom_call_target="tpu_custom_call" | custom-call | flops 9200000000 | bytes 1 | tf_op jit(solution)/shard_map/heads_finish_heads/pallas_call | solution.py:125
  (205 shorter events, 30.8 us)
Async XLA Ops:
  0.7 18.1 %collective-permute-start.2 = (bf16[768,1536]{1,0:T(8,128)(2,1)}, bf16[768,1536]{1,0:T(8,128)(2,1)S(1)}, u32[]{:S(2)}, u32[]{:S(2)}) collective-permute-start(bf16[768,1536]{1,0:T(8,128)(2,1)} %refs_4_.5), channel_id=1, source_target_pairs={{0,1},{1,0},{2,3},{3,2},{4,5},{5,4},{6,7},{7,6},{8,9},{9,8},{10,11... | collective-permute-start | bytes 7077896 | tf_op jit(solution)/shard_map/ppermute | solution.py:43
  1.2 17.6 %collective-permute-start.3 = (bf16[1536,768]{1,0:T(8,128)(2,1)}, bf16[1536,768]{1,0:T(8,128)(2,1)}, u32[]{:S(2)}, u32[]{:S(2)}) collective-permute-start(bf16[1536,768]{1,0:T(8,128)(2,1)} %refs_2_.9), channel_id=1, source_target_pairs={{0,1},{1,0},{2,3},{3,2},{4,5},{5,4},{6,7},{7,6},{8,9},{9,8},{10,11... | collective-permute-start | bytes 7077896 | tf_op jit(solution)/shard_map/ppermute | solution.py:43
  1.4 10.1 %copy-start.44 = (s32[8]{0:T(128)S(1)}, s32[8]{0:T(128)}, u32[]{:S(2)}) copy-start(s32[8]{0:T(128)} %param.27) | copy-start | bytes 100
  1.4 10.2 %copy-start.10 = (bf16[1024,768]{1,0:T(8,128)(2,1)S(1)}, bf16[1024,768]{1,0:T(8,128)(2,1)}, u32[]{:S(2)}) copy-start(bf16[1024,768]{1,0:T(8,128)(2,1)} %refs_1_.5) | copy-start | bytes 4718596
  1.4 10.2 %copy-start.12 = (bf16[768,384]{1,0:T(8,128)(2,1)S(1)}, bf16[768,384]{1,0:T(8,128)(2,1)}, u32[]{:S(2)}) copy-start(bf16[768,384]{1,0:T(8,128)(2,1)} %refs_9_.5) | copy-start | bytes 1769476
  1.5 10.2 %copy-start.13 = (bf16[768,384]{1,0:T(8,128)(2,1)S(1)}, bf16[768,384]{1,0:T(8,128)(2,1)}, u32[]{:S(2)}) copy-start(bf16[768,384]{1,0:T(8,128)(2,1)} %refs_10_.3) | copy-start | bytes 1769476
  1.5 10.2 %copy-start.15 = (bf16[768,384]{1,0:T(8,128)(2,1)S(1)}, bf16[768,384]{1,0:T(8,128)(2,1)}, u32[]{:S(2)}) copy-start(bf16[768,384]{1,0:T(8,128)(2,1)} %refs_11_.3) | copy-start | bytes 1769476
  1.5 10.2 %copy-start.21 = (s32[2,512]{1,0:T(2,128)S(1)}, s32[2,512]{1,0:T(2,128)}, u32[]{:S(2)}) copy-start(s32[2,512]{1,0:T(2,128)} %refs_7_.3) | copy-start | bytes 12292
  1.5 10.2 %copy-start.22 = (s32[2,512]{1,0:T(2,128)S(1)}, s32[2,512]{1,0:T(2,128)}, u32[]{:S(2)}) copy-start(s32[2,512]{1,0:T(2,128)} %refs_8_.4) | copy-start | bytes 12292
  1.5 10.2 %copy-start.23 = (bf16[384]{0:T(512)(128)(2,1)S(1)}, bf16[384]{0:T(512)(128)(2,1)}, u32[]{:S(2)}) copy-start(bf16[384]{0:T(512)(128)(2,1)} %refs_5_.3) | copy-start | bytes 2308
  1.5 10.1 %copy-start.24 = (bf16[384]{0:T(512)(128)(2,1)S(1)}, bf16[384]{0:T(512)(128)(2,1)}, u32[]{:S(2)}) copy-start(bf16[384]{0:T(512)(128)(2,1)} %refs_6_.3) | copy-start | bytes 2308
  10.5 8.3 %collective-permute-start = (bf16[384,512]{1,0:T(8,128)(2,1)}, bf16[384,512]{1,0:T(8,128)(2,1)}, u32[]{:S(2)}, u32[]{:S(2)}) collective-permute-start(bf16[384,512]{1,0:T(8,128)(2,1)} %get-tuple-element.115.refs_8_.refs_5_), channel_id=1, source_target_pairs={{0,1},{1,0},{2,3},{3,2},{4,5},{5,4},{6,7},{7,6},{8,9},{9,8},{10,11... | collective-permute-start | bytes 1179656 | tf_op jit(solution)/shard_map/ppermute | solution.py:43
  11.0 7.8 %collective-permute-start.1 = (bf16[384,768]{1,0:T(8,128)(2,1)}, bf16[384,768]{1,0:T(8,128)(2,1)}, u32[]{:S(2)}, u32[]{:S(2)}) collective-permute-start(bf16[384,768]{1,0:T(8,128)(2,1)} %refs_2_.11), channel_id=1, source_target_pairs={{0,1},{1,0},{2,3},{3,2},{4,5},{5,4},{6,7},{7,6},{8,9},{9,8},{10,11... | collective-permute-start | bytes 1769480 | tf_op jit(solution)/shard_map/ppermute | solution.py:43
  11.1 7.7 %collective-permute-start.4 = (bf16[1,1536]{1,0:T(2,128)(2,1)S(1)}, bf16[1,1536]{1,0:T(2,128)(2,1)S(1)}, u32[]{:S(2)}, u32[]{:S(2)}) collective-permute-start(bf16[1,1536]{1,0:T(2,128)(2,1)S(1)} %convert_element_type.23), channel_id=1, source_target_pairs={{0,1},{1,0},{2,3},{3,2},{4,5},{5,4},{6,7},{7,6},{8,9},{9,8},{10,11... | collective-permute-start | bytes 9224 | tf_op jit(solution)/shard_map/ppermute | solution.py:43
  32.0 27.8 %collective-permute-start.13 = (bf16[512,1536]{1,0:T(8,128)(2,1)}, bf16[512,1536]{1,0:T(8,128)(2,1)}, u32[]{:S(2)}, u32[]{:S(2)}) collective-permute-start(bf16[512,1536]{1,0:T(8,128)(2,1)} %get-tuple-element.125), channel_id=1, source_target_pairs={{0,1},{1,0},{2,3},{3,2},{4,5},{5,4},{6,7},{7,6},{8,9},{9,8},{10,11... | collective-permute-start | bytes 4718600 | tf_op jit(solution)/shard_map/ppermute | solution.py:43
  32.2 4.7 %collective-permute-start.5 = (bf16[8,896]{1,0:T(8,128)(2,1)S(1)}, bf16[8,896]{1,0:T(8,128)(2,1)S(1)}, u32[]{:S(2)}, u32[]{:S(2)}) collective-permute-start(bf16[8,896]{1,0:T(8,128)(2,1)S(1)} %pad_maximum_fusion), channel_id=1, source_target_pairs={{0,2},{2,0},{4,6},{6,4},{8,10},{10,8},{12,14},{14,12},{16,18},{18,... | collective-permute-start | bytes 43016 | tf_op jit(solution)/shard_map/ppermute | solution.py:43
  35.2 3.7 %collective-permute-start.6 = (bf16[8,896]{1,0:T(8,128)(2,1)S(1)}, bf16[8,896]{1,0:T(8,128)(2,1)S(1)}, u32[]{:S(2)}, u32[]{:S(2)}) collective-permute-start(bf16[8,896]{1,0:T(8,128)(2,1)S(1)} %pad_maximum_fusion), channel_id=1, source_target_pairs={{0,4},{2,6},{4,0},{6,2},{8,12},{10,14},{12,8},{14,10},{16,20},{18,... | collective-permute-start | bytes 43016 | tf_op jit(solution)/shard_map/ppermute | solution.py:43
  36.7 4.6 %collective-permute-start.7 = (bf16[8,896]{1,0:T(8,128)(2,1)S(1)}, bf16[8,896]{1,0:T(8,128)(2,1)S(1)}, u32[]{:S(2)}, u32[]{:S(2)}) collective-permute-start(bf16[8,896]{1,0:T(8,128)(2,1)S(1)} %pad_maximum_fusion), channel_id=1, source_target_pairs={{0,6},{2,4},{4,2},{6,0},{8,14},{10,12},{12,10},{14,8},{16,22},{18,... | collective-permute-start | bytes 43016 | tf_op jit(solution)/shard_map/ppermute | solution.py:43
  41.4 6.1 %collective-permute-start.10 = (bf16[32,896]{1,0:T(8,128)(2,1)S(1)}, bf16[32,896]{1,0:T(8,128)(2,1)S(1)}, u32[]{:S(2)}, u32[]{:S(2)}) collective-permute-start(bf16[32,896]{1,0:T(8,128)(2,1)S(1)} %concatenate.27), channel_id=1, source_target_pairs={{0,24},{2,26},{4,28},{6,30},{8,16},{10,18},{12,20},{14,22},{16,8},... | collective-permute-start | bytes 172040 | tf_op jit(solution)/shard_map/ppermute | solution.py:43
  45.0 4.2 %collective-permute-start.8 = (bf16[32,896]{1,0:T(8,128)(2,1)S(1)}, bf16[32,896]{1,0:T(8,128)(2,1)S(1)}, u32[]{:S(2)}, u32[]{:S(2)}) collective-permute-start(bf16[32,896]{1,0:T(8,128)(2,1)S(1)} %concatenate.27), channel_id=1, source_target_pairs={{0,8},{2,10},{4,12},{6,14},{8,0},{10,2},{12,4},{14,6},{16,24},{18,... | collective-permute-start | bytes 172040 | tf_op jit(solution)/shard_map/ppermute | solution.py:43
  45.0 5.1 %collective-permute-start.9 = (bf16[32,896]{1,0:T(8,128)(2,1)S(1)}, bf16[32,896]{1,0:T(8,128)(2,1)S(1)}, u32[]{:S(2)}, u32[]{:S(2)}) collective-permute-start(bf16[32,896]{1,0:T(8,128)(2,1)S(1)} %concatenate.27), channel_id=1, source_target_pairs={{0,16},{2,18},{4,20},{6,22},{8,24},{10,26},{12,28},{14,30},{16,0},... | collective-permute-start | bytes 172040 | tf_op jit(solution)/shard_map/ppermute | solution.py:43
  50.2 1.6 collective-permute-start.11
  55.4 4.4 %collective-permute-start.12 = (bf16[512,768]{1,0:T(8,128)(2,1)S(1)}, bf16[512,768]{1,0:T(8,128)(2,1)S(1)}, u32[]{:S(2)}, u32[]{:S(2)}) collective-permute-start(bf16[512,768]{1,0:T(8,128)(2,1)S(1)} %get-tuple-element.121.refs_1_), channel_id=1, source_target_pairs={{0,1},{1,0},{2,3},{3,2},{4,5},{5,4},{6,7},{7,6},{8,9},{9,8},{10,11... | collective-permute-start | bytes 2359304 | tf_op jit(solution)/shard_map/ppermute | solution.py:43
  59.2 12.5 %collective-permute-start.16 = (bf16[512,1536]{1,0:T(8,128)(2,1)S(1)}, bf16[512,1536]{1,0:T(8,128)(2,1)S(1)}, u32[]{:S(2)}, u32[]{:S(2)}) collective-permute-start(bf16[512,1536]{1,0:T(8,128)(2,1)S(1)} %unit_back_far.1.refs_5_.refs_1_), channel_id=1, source_target_pairs={{0,1},{1,0},{2,3},{3,2},{4,5},{5,4},{6,7},{7,6},{8,9},{9,8},{10,11... | collective-permute-start | bytes 4718600 | tf_op jit(solution)/shard_map/ppermute | solution.py:43
  59.7 12.1 %collective-permute-start.17 = (bf16[512,768]{1,0:T(8,128)(2,1)S(1)}, bf16[512,768]{1,0:T(8,128)(2,1)S(1)}, u32[]{:S(2)}, u32[]{:S(2)}) collective-permute-start(bf16[512,768]{1,0:T(8,128)(2,1)S(1)} %copy-done.6), channel_id=1, source_target_pairs={{0,1},{1,0},{2,3},{3,2},{4,5},{5,4},{6,7},{7,6},{8,9},{9,8},{10,11... | collective-permute-start | bytes 2359304 | tf_op jit(solution)/shard_map/ppermute | solution.py:43
  70.3 2.4 %collective-permute-start.18 = (bf16[512,768]{1,0:T(8,128)(2,1)S(1)}, bf16[512,768]{1,0:T(8,128)(2,1)S(1)}, u32[]{:S(2)}, u32[]{:S(2)}) collective-permute-start(bf16[512,768]{1,0:T(8,128)(2,1)S(1)} %get-tuple-element.132.refs_5_.refs_1_), channel_id=1, source_target_pairs={{0,1},{1,0},{2,3},{3,2},{4,5},{5,4},{6,7},{7,6},{8,9},{9,8},{10,11... | collective-permute-start | bytes 2359304 | tf_op jit(solution)/shard_map/ppermute | solution.py:43
  70.7 15.4 %collective-permute-start.14 = (bf16[384,768]{1,0:T(8,128)(2,1)S(1)}, bf16[384,768]{1,0:T(8,128)(2,1)S(1)}, u32[]{:S(2)}, u32[]{:S(2)}) collective-permute-start(bf16[384,768]{1,0:T(8,128)(2,1)S(1)} %get-tuple-element.139), channel_id=1, source_target_pairs={{0,2},{2,0},{4,6},{6,4},{8,10},{10,8},{12,14},{14,12},{16,18},{18,... | collective-permute-start | bytes 1769480 | tf_op jit(solution)/shard_map/ppermute | solution.py:43
  71.3 15.1 %collective-permute-start.15 = (bf16[384,768]{1,0:T(8,128)(2,1)S(1)}, bf16[384,768]{1,0:T(8,128)(2,1)S(1)}, u32[]{:S(2)}, u32[]{:S(2)}) collective-permute-start(bf16[384,768]{1,0:T(8,128)(2,1)S(1)} %get-tuple-element.140), channel_id=1, source_target_pairs={{0,4},{2,6},{4,0},{6,2},{8,12},{10,14},{12,8},{14,10},{16,20},{18,... | collective-permute-start | bytes 1769480 | tf_op jit(solution)/shard_map/ppermute | solution.py:43
  71.8 46.4 %collective-permute-start.22 = (f32[8,768]{1,0:T(8,128)S(1)}, f32[8,768]{1,0:T(8,128)S(1)}, u32[]{:S(2)}, u32[]{:S(2)}) collective-permute-start(f32[8,768]{1,0:T(8,128)S(1)} %get-tuple-element.142.refs_9_.refs_8_), channel_id=1, source_target_pairs={{0,1},{1,0},{2,3},{3,2},{4,5},{5,4},{6,7},{7,6},{8,9},{9,8},{10,11... | collective-permute-start | bytes 73736 | tf_op jit(solution)/shard_map/ppermute | solution.py:43
  87.3 10.9 %collective-permute-start.19 = (bf16[192,768]{1,0:T(8,128)(2,1)S(1)}, bf16[192,768]{1,0:T(8,128)(2,1)S(1)}, u32[]{:S(2)}, u32[]{:S(2)}) collective-permute-start(bf16[192,768]{1,0:T(8,128)(2,1)S(1)} %get-tuple-element.152), channel_id=1, source_target_pairs={{0,4},{2,6},{4,0},{6,2},{8,12},{10,14},{12,8},{14,10},{16,20},{18,... | collective-permute-start | bytes 884744 | tf_op jit(solution)/shard_map/ppermute | solution.py:43
  87.8 10.4 %collective-permute-start.20 = (bf16[192,768]{1,0:T(8,128)(2,1)S(1)}, bf16[192,768]{1,0:T(8,128)(2,1)S(1)}, u32[]{:S(2)}, u32[]{:S(2)}) collective-permute-start(bf16[192,768]{1,0:T(8,128)(2,1)S(1)} %get-tuple-element.153), channel_id=1, source_target_pairs={{0,2},{2,0},{4,6},{6,4},{8,10},{10,8},{12,14},{14,12},{16,18},{18,... | collective-permute-start | bytes 884744 | tf_op jit(solution)/shard_map/ppermute | solution.py:43
  89.3 23.1 %collective-permute-start.24 = (bf16[384,1024]{1,0:T(8,128)(2,1)S(1)}, bf16[384,1024]{1,0:T(8,128)(2,1)S(1)}, u32[]{:S(2)}, u32[]{:S(2)}) collective-permute-start(bf16[384,1024]{1,0:T(8,128)(2,1)S(1)} %get-tuple-element.164), channel_id=1, source_target_pairs={{0,2},{2,0},{4,6},{6,4},{8,10},{10,8},{12,14},{14,12},{16,18},{18,... | collective-permute-start | bytes 2359304 | tf_op jit(solution)/shard_map/ppermute | solution.py:43
  89.8 20.2 %collective-permute-start.25 = (bf16[384,896]{1,0:T(8,128)(2,1)S(1)}, bf16[384,896]{1,0:T(8,128)(2,1)S(1)}, u32[]{:S(2)}, u32[]{:S(2)}) collective-permute-start(bf16[384,896]{1,0:T(8,128)(2,1)S(1)} %get-tuple-element.166), channel_id=1, source_target_pairs={{0,4},{2,6},{4,0},{6,2},{8,12},{10,14},{12,8},{14,10},{16,20},{18,... | collective-permute-start | bytes 2064392 | tf_op jit(solution)/shard_map/ppermute | solution.py:43
  98.9 14.3 %collective-permute-start.23 = (bf16[96,1536]{1,0:T(8,128)(2,1)S(1)}, bf16[96,1536]{1,0:T(8,128)(2,1)S(1)}, u32[]{:S(2)}, u32[]{:S(2)}) collective-permute-start(bf16[96,1536]{1,0:T(8,128)(2,1)S(1)} %get-tuple-element.162), channel_id=1, source_target_pairs={{0,8},{2,10},{4,12},{6,14},{8,0},{10,2},{12,4},{14,6},{16,24},{18,... | collective-permute-start | bytes 884744 | tf_op jit(solution)/shard_map/ppermute | solution.py:43
  108.0 15.7 %collective-permute-start.21 = (bf16[512,768]{1,0:T(8,128)(2,1)S(1)}, bf16[512,768]{1,0:T(8,128)(2,1)S(1)}, u32[]{:S(2)}, u32[]{:S(2)}) collective-permute-start(bf16[512,768]{1,0:T(8,128)(2,1)S(1)} %get-tuple-element.155.refs_5_), channel_id=1, source_target_pairs={{0,1},{1,0},{2,3},{3,2},{4,5},{5,4},{6,7},{7,6},{8,9},{9,8},{10,11... | collective-permute-start | bytes 2359304 | tf_op jit(solution)/shard_map/ppermute | solution.py:43
  113.9 8.3 %collective-permute-start.30 = (bf16[48,1536]{1,0:T(8,128)(2,1)S(1)}, bf16[48,1536]{1,0:T(8,128)(2,1)S(1)}, u32[]{:S(2)}, u32[]{:S(2)}) collective-permute-start(bf16[48,1536]{1,0:T(8,128)(2,1)S(1)} %get-tuple-element.176), channel_id=1, source_target_pairs={{0,16},{2,18},{4,20},{6,22},{8,24},{10,26},{12,28},{14,30},{16,0},... | collective-permute-start | bytes 442376 | tf_op jit(solution)/shard_map/ppermute | solution.py:43
  115.2 11.7 %collective-permute-start.28 = (bf16[192,1024]{1,0:T(8,128)(2,1)S(1)}, bf16[192,1024]{1,0:T(8,128)(2,1)S(1)}, u32[]{:S(2)}, u32[]{:S(2)}) collective-permute-start(bf16[192,1024]{1,0:T(8,128)(2,1)S(1)} %get-tuple-element.174), channel_id=1, source_target_pairs={{0,4},{2,6},{4,0},{6,2},{8,12},{10,14},{12,8},{14,10},{16,20},{18,... | collective-permute-start | bytes 1179656 | tf_op jit(solution)/shard_map/ppermute | solution.py:43
  116.7 10.1 %collective-permute-start.29 = (bf16[192,896]{1,0:T(8,128)(2,1)S(1)}, bf16[192,896]{1,0:T(8,128)(2,1)S(1)}, u32[]{:S(2)}, u32[]{:S(2)}) collective-permute-start(bf16[192,896]{1,0:T(8,128)(2,1)S(1)} %get-tuple-element.175), channel_id=1, source_target_pairs={{0,2},{2,0},{4,6},{6,4},{8,10},{10,8},{12,14},{14,12},{16,18},{18,... | collective-permute-start | bytes 1032200 | tf_op jit(solution)/shard_map/ppermute | solution.py:43
  121.6 13.4 %collective-permute-start.26 = (bf16[400,640]{1,0:T(8,128)(2,1)S(1)}, bf16[400,640]{1,0:T(8,128)(2,1)S(1)}, u32[]{:S(2)}, u32[]{:S(2)}) collective-permute-start(bf16[400,640]{1,0:T(8,128)(2,1)S(1)} %get-tuple-element.170), channel_id=1, source_target_pairs={{0,2},{2,0},{4,6},{6,4},{8,10},{10,8},{12,14},{14,12},{16,18},{18,... | collective-permute-start | bytes 1536008 | tf_op jit(solution)/shard_map/ppermute | solution.py:43
  122.2 10.0 %collective-permute-start.27 = (bf16[384,512]{1,0:T(8,128)(2,1)S(1)}, bf16[384,512]{1,0:T(8,128)(2,1)S(1)}, u32[]{:S(2)}, u32[]{:S(2)}) collective-permute-start(bf16[384,512]{1,0:T(8,128)(2,1)S(1)} %get-tuple-element.172), channel_id=1, source_target_pairs={{0,4},{2,6},{4,0},{6,2},{8,12},{10,14},{12,8},{14,10},{16,20},{18,... | collective-permute-start | bytes 1179656 | tf_op jit(solution)/shard_map/ppermute | solution.py:43
  123.8 13.9 %collective-permute-start.34 = (bf16[48,1536]{1,0:T(8,128)(2,1)S(1)}, bf16[48,1536]{1,0:T(8,128)(2,1)S(1)}, u32[]{:S(2)}, u32[]{:S(2)}) collective-permute-start(bf16[48,1536]{1,0:T(8,128)(2,1)S(1)} %down_add_last.1.refs_5_.refs_1_), channel_id=1, source_target_pairs={{0,16},{2,18},{4,20},{6,22},{8,24},{10,26},{12,28},{14,30},{16,0},... | collective-permute-start | bytes 442376 | tf_op jit(solution)/shard_map/ppermute | solution.py:43
  127.6 11.8 %collective-permute-start.33 = (bf16[96,1920]{1,0:T(8,128)(2,1)S(1)}, bf16[96,1920]{1,0:T(8,128)(2,1)S(1)}, u32[]{:S(2)}, u32[]{:S(2)}) collective-permute-start(bf16[96,1920]{1,0:T(8,128)(2,1)S(1)} %get-tuple-element.182), channel_id=1, source_target_pairs={{0,8},{2,10},{4,12},{6,14},{8,0},{10,2},{12,4},{14,6},{16,24},{18,... | collective-permute-start | bytes 1105928 | tf_op jit(solution)/shard_map/ppermute | solution.py:43
  135.7 7.0 %collective-permute-start.31 = (bf16[208,640]{1,0:T(8,128)(2,1)S(1)}, bf16[208,640]{1,0:T(8,128)(2,1)S(1)}, u32[]{:S(2)}, u32[]{:S(2)}) collective-permute-start(bf16[208,640]{1,0:T(8,128)(2,1)S(1)} %get-tuple-element.179), channel_id=1, source_target_pairs={{0,4},{2,6},{4,0},{6,2},{8,12},{10,14},{12,8},{14,10},{16,20},{18,... | collective-permute-start | bytes 798728 | tf_op jit(solution)/shard_map/ppermute | solution.py:43
  136.3 6.5 %collective-permute-start.32 = (bf16[192,512]{1,0:T(8,128)(2,1)S(1)}, bf16[192,512]{1,0:T(8,128)(2,1)S(1)}, u32[]{:S(2)}, u32[]{:S(2)}) collective-permute-start(bf16[192,512]{1,0:T(8,128)(2,1)S(1)} %get-tuple-element.181), channel_id=1, source_target_pairs={{0,2},{2,0},{4,6},{6,4},{8,10},{10,8},{12,14},{14,12},{16,18},{18,... | collective-permute-start | bytes 589832 | tf_op jit(solution)/shard_map/ppermute | solution.py:43
  138.3 11.7 %collective-permute-start.37 = (bf16[96,1536]{1,0:T(8,128)(2,1)S(1)}, bf16[96,1536]{1,0:T(8,128)(2,1)S(1)}, u32[]{:S(2)}, u32[]{:S(2)}) collective-permute-start(bf16[96,1536]{1,0:T(8,128)(2,1)S(1)} %down_join_pieces.1.refs_3_.refs_1_), channel_id=1, source_target_pairs={{0,8},{2,10},{4,12},{6,14},{8,0},{10,2},{12,4},{14,6},{16,24},{18,... | collective-permute-start | bytes 884744 | tf_op jit(solution)/shard_map/ppermute | solution.py:43
  140.1 14.9 %collective-permute-start.36 = (bf16[48,1920]{1,0:T(8,128)(2,1)S(1)}, bf16[48,1920]{1,0:T(8,128)(2,1)S(1)}, u32[]{:S(2)}, u32[]{:S(2)}) collective-permute-start(bf16[48,1920]{1,0:T(8,128)(2,1)S(1)} %get-tuple-element.186), channel_id=1, source_target_pairs={{0,16},{2,18},{4,20},{6,22},{8,24},{10,26},{12,28},{14,30},{16,0},... | collective-permute-start | bytes 552968 | tf_op jit(solution)/shard_map/ppermute | solution.py:43
  143.5 12.4 %collective-permute-start.35 = (bf16[112,1152]{1,0:T(8,128)(2,1)S(1)}, bf16[112,1152]{1,0:T(8,128)(2,1)S(1)}, u32[]{:S(2)}, u32[]{:S(2)}) collective-permute-start(bf16[112,1152]{1,0:T(8,128)(2,1)S(1)} %get-tuple-element.185), channel_id=1, source_target_pairs={{0,8},{2,10},{4,12},{6,14},{8,0},{10,2},{12,4},{14,6},{16,24},{18,... | collective-permute-start | bytes 774152 | tf_op jit(solution)/shard_map/ppermute | solution.py:43
  150.6 15.7 %collective-permute-start.39 = (bf16[192,768]{1,0:T(8,128)(2,1)S(1)}, bf16[192,768]{1,0:T(8,128)(2,1)S(1)}, u32[]{:S(2)}, u32[]{:S(2)}) collective-permute-start(bf16[192,768]{1,0:T(8,128)(2,1)S(1)} %get-tuple-element.190.refs_1_), channel_id=1, source_target_pairs={{0,4},{2,6},{4,0},{6,2},{8,12},{10,14},{12,8},{14,10},{16,20},{18,... | collective-permute-start | bytes 884744 | tf_op jit(solution)/shard_map/ppermute | solution.py:43
  153.0 13.2 %collective-permute-start.40 = (bf16[192,768]{1,0:T(8,128)(2,1)S(1)}, bf16[192,768]{1,0:T(8,128)(2,1)S(1)}, u32[]{:S(2)}, u32[]{:S(2)}) collective-permute-start(bf16[192,768]{1,0:T(8,128)(2,1)S(1)} %get-tuple-element.187.refs_3_), channel_id=1, source_target_pairs={{0,2},{2,0},{4,6},{6,4},{8,10},{10,8},{12,14},{14,12},{16,18},{18,... | collective-permute-start | bytes 884744 | tf_op jit(solution)/shard_map/ppermute | solution.py:43
  155.6 9.9 %collective-permute-start.41 = (bf16[48,1920]{1,0:T(8,128)(2,1)S(1)}, bf16[48,1920]{1,0:T(8,128)(2,1)S(1)}, u32[]{:S(2)}, u32[]{:S(2)}) collective-permute-start(bf16[48,1920]{1,0:T(8,128)(2,1)S(1)} %up_add_last.1.refs_3_.refs_1_), channel_id=1, source_target_pairs={{0,16},{2,18},{4,20},{6,22},{8,24},{10,26},{12,28},{14,30},{16,0},... | collective-permute-start | bytes 552968 | tf_op jit(solution)/shard_map/ppermute | solution.py:43
  156.5 12.7 %collective-permute-start.38 = (bf16[64,1152]{1,0:T(8,128)(2,1)S(1)}, bf16[64,1152]{1,0:T(8,128)(2,1)S(1)}, u32[]{:S(2)}, u32[]{:S(2)}) collective-permute-start(bf16[64,1152]{1,0:T(8,128)(2,1)S(1)} %get-tuple-element.189), channel_id=1, source_target_pairs={{0,16},{2,18},{4,20},{6,22},{8,24},{10,26},{12,28},{14,30},{16,0},... | collective-permute-start | bytes 442376 | tf_op jit(solution)/shard_map/ppermute | solution.py:43
  166.1 7.6 %collective-permute-start.43 = (bf16[96,1920]{1,0:T(8,128)(2,1)S(1)}, bf16[96,1920]{1,0:T(8,128)(2,1)S(1)}, u32[]{:S(2)}, u32[]{:S(2)}) collective-permute-start(bf16[96,1920]{1,0:T(8,128)(2,1)S(1)} %up_join_pieces.1.refs_5_.refs_1_), channel_id=1, source_target_pairs={{0,8},{2,10},{4,12},{6,14},{8,0},{10,2},{12,4},{14,6},{16,24},{18,... | collective-permute-start | bytes 1105928 | tf_op jit(solution)/shard_map/ppermute | solution.py:43
  166.9 27.3 %collective-permute-start.49 = (bf16[384,768]{1,0:T(8,128)(2,1)S(1)}, bf16[384,768]{1,0:T(8,128)(2,1)S(1)}, u32[]{:S(2)}, u32[]{:S(2)}) collective-permute-start(bf16[384,768]{1,0:T(8,128)(2,1)S(1)} %get-tuple-element.199.refs_1_), channel_id=1, source_target_pairs={{0,2},{2,0},{4,6},{6,4},{8,10},{10,8},{12,14},{14,12},{16,18},{18,... | collective-permute-start | bytes 1769480 | tf_op jit(solution)/shard_map/ppermute | solution.py:43
  166.9 28.0 %collective-permute-start.50 = (bf16[384,768]{1,0:T(8,128)(2,1)S(1)}, bf16[384,768]{1,0:T(8,128)(2,1)S(1)}, u32[]{:S(2)}, u32[]{:S(2)}) collective-permute-start(bf16[384,768]{1,0:T(8,128)(2,1)S(1)} %get-tuple-element.191.refs_3_), channel_id=1, source_target_pairs={{0,4},{2,6},{4,0},{6,2},{8,12},{10,14},{12,8},{14,10},{16,20},{18,... | collective-permute-start | bytes 1769480 | tf_op jit(solution)/shard_map/ppermute | solution.py:43
  169.8 7.1 %collective-permute-start.42 = (bf16[48,1152]{1,0:T(8,128)(2,1)S(1)}, bf16[48,1152]{1,0:T(8,128)(2,1)S(1)}, u32[]{:S(2)}, u32[]{:S(2)}) collective-permute-start(bf16[48,1152]{1,0:T(8,128)(2,1)S(1)} %get-tuple-element.192.refs_1_), channel_id=1, source_target_pairs={{0,16},{2,18},{4,20},{6,22},{8,24},{10,26},{12,28},{14,30},{16,0},... | collective-permute-start | bytes 331784 | tf_op jit(solution)/shard_map/ppermute | solution.py:43
  175.1 12.5 %collective-permute-start.45 = (bf16[192,1024]{1,0:T(8,128)(2,1)S(1)}, bf16[192,1024]{1,0:T(8,128)(2,1)S(1)}, u32[]{:S(2)}, u32[]{:S(2)}) collective-permute-start(bf16[192,1024]{1,0:T(8,128)(2,1)S(1)} %get-tuple-element.195.refs_1_), channel_id=1, source_target_pairs={{0,4},{2,6},{4,0},{6,2},{8,12},{10,14},{12,8},{14,10},{16,20},{18,... | collective-permute-start | bytes 1179656 | tf_op jit(solution)/shard_map/ppermute | solution.py:43
  175.1 9.2 %collective-permute-start.46 = (bf16[192,896]{1,0:T(8,128)(2,1)}, bf16[192,896]{1,0:T(8,128)(2,1)}, u32[]{:S(2)}, u32[]{:S(2)}) collective-permute-start(bf16[192,896]{1,0:T(8,128)(2,1)} %get-tuple-element.194.refs_3_), channel_id=1, source_target_pairs={{0,2},{2,0},{4,6},{6,4},{8,10},{10,8},{12,14},{14,12},{16,18},{18,... | collective-permute-start | bytes 1032200 | tf_op jit(solution)/shard_map/ppermute | solution.py:43
  179.1 9.8 %collective-permute-start.44 = (bf16[96,1152]{1,0:T(8,128)(2,1)S(1)}, bf16[96,1152]{1,0:T(8,128)(2,1)}, u32[]{:S(2)}, u32[]{:S(2)}) collective-permute-start(bf16[96,1152]{1,0:T(8,128)(2,1)S(1)} %heads_join_pieces.1.refs_5_.refs_1_), channel_id=1, source_target_pairs={{0,8},{2,10},{4,12},{6,14},{8,0},{10,2},{12,4},{14,6},{16,24},{18,... | collective-permute-start | bytes 663560 | tf_op jit(solution)/shard_map/ppermute | solution.py:43
  188.8 21.0 %collective-permute-start.54 = (bf16[384,896]{1,0:T(8,128)(2,1)S(1)}, bf16[384,896]{1,0:T(8,128)(2,1)S(1)}, u32[]{:S(2)}, u32[]{:S(2)}) collective-permute-start(bf16[384,896]{1,0:T(8,128)(2,1)S(1)} %get-tuple-element.196.refs_3_), channel_id=1, source_target_pairs={{0,4},{2,6},{4,0},{6,2},{8,12},{10,14},{12,8},{14,10},{16,20},{18,... | collective-permute-start | bytes 2064392 | tf_op jit(solution)/shard_map/ppermute | solution.py:43
  190.8 18.2 %collective-permute-start.47 = (bf16[192,640]{1,0:T(8,128)(2,1)S(1)}, bf16[192,640]{1,0:T(8,128)(2,1)S(1)}, u32[]{:S(2)}, u32[]{:S(2)}) collective-permute-start(bf16[192,640]{1,0:T(8,128)(2,1)S(1)} %get-tuple-element.197.refs_1_), channel_id=1, source_target_pairs={{0,4},{2,6},{4,0},{6,2},{8,12},{10,14},{12,8},{14,10},{16,20},{18,... | collective-permute-start | bytes 737288 | tf_op jit(solution)/shard_map/ppermute | solution.py:43
  192.9 6.2 %collective-permute-start.48 = (bf16[192,512]{1,0:T(8,128)(2,1)S(1)}, bf16[192,512]{1,0:T(8,128)(2,1)S(1)}, u32[]{:S(2)}, u32[]{:S(2)}) collective-permute-start(bf16[192,512]{1,0:T(8,128)(2,1)S(1)} %get-tuple-element.198.refs_5_.refs_3_), channel_id=1, source_target_pairs={{0,2},{2,0},{4,6},{6,4},{8,10},{10,8},{12,14},{14,12},{16,18},{18,... | collective-permute-start | bytes 589832 | tf_op jit(solution)/shard_map/ppermute | solution.py:43
  194.2 18.6 %collective-permute-start.53 = (bf16[384,1024]{1,0:T(8,128)(2,1)S(1)}, bf16[384,1024]{1,0:T(8,128)(2,1)S(1)}, u32[]{:S(2)}, u32[]{:S(2)}) collective-permute-start(bf16[384,1024]{1,0:T(8,128)(2,1)S(1)} %get-tuple-element.203.refs_1_), channel_id=1, source_target_pairs={{0,2},{2,0},{4,6},{6,4},{8,10},{10,8},{12,14},{14,12},{16,18},{18,... | collective-permute-start | bytes 2359304 | tf_op jit(solution)/shard_map/ppermute | solution.py:43
  209.6 8.9 %collective-permute-start.51 = (bf16[384,640]{1,0:T(8,128)(2,1)S(1)}, bf16[384,640]{1,0:T(8,128)(2,1)S(1)}, u32[]{:S(2)}, u32[]{:S(2)}) collective-permute-start(bf16[384,640]{1,0:T(8,128)(2,1)S(1)} %get-tuple-element.201.refs_1_), channel_id=1, source_target_pairs={{0,2},{2,0},{4,6},{6,4},{8,10},{10,8},{12,14},{14,12},{16,18},{18,... | collective-permute-start | bytes 1474568 | tf_op jit(solution)/shard_map/ppermute | solution.py:43
  209.7 7.8 %collective-permute-start.52 = (bf16[384,512]{1,0:T(8,128)(2,1)S(1)}, bf16[384,512]{1,0:T(8,128)(2,1)S(1)}, u32[]{:S(2)}, u32[]{:S(2)}) collective-permute-start(bf16[384,512]{1,0:T(8,128)(2,1)S(1)} %get-tuple-element.202.refs_5_.refs_3_), channel_id=1, source_target_pairs={{0,4},{2,6},{4,0},{6,2},{8,12},{10,14},{12,8},{14,10},{16,20},{18,... | collective-permute-start | bytes 1179656 | tf_op jit(solution)/shard_map/ppermute | solution.py:43
  (36 other events, 159.7 us)
